TPU v7x, 256 devices: a whole 4x4x8 slice. The times are simulated.
256 devices in a mesh: seq: 32 (over y, z_hi, x), tp: 8 (over z_lo, core).
Axes of the slice: x: 4, y: 4, z: 8 (z_hi: 2, z_lo: 4; z = z_hi * 4 + z_lo), core: 2. Of those that a mesh axis runs over, the one named last changes fastest.
Arguments:
- video_qkv: bfloat16 [8, 32, 2048, 3, 128], P(None, 'tp', 'seq'), may hold values from -110 to 110
- cross_query: bfloat16 [8, 32, 2048, 128], P(None, 'tp', 'seq'), may hold values from -110 to 110
- captions: bfloat16 [8, 192, 4096], P(None, 'tp', 'seq'), may hold values from -700 to 700
- caption_gain: float32 [4096], P('seq'), may hold values from 0.1 to 1.9
- key_value_weight: bfloat16 [4096, 2, 32, 128], P('seq'), may hold values from -0.09375 to 0.09375
- caption_lengths: int32 [8], replicated, may hold values from 1 to 192, 960 in all
Outputs:
- self_out: bfloat16 [8, 32, 2048, 128], P(None, 'tp', 'seq')
- cross_out: bfloat16 [8, 32, 2048, 128], P(None, 'tp', 'seq')
Inputs may be any that keep to these rules, and one draw needn't show every extreme that they name: `caption_lengths`: the lengths sum to 960; the longest is exactly 192.
All inputs are finite; a program needn't handle non-finite values.
Results may differ from a plain program's by a relative error of at most 0.012.
The roundings to bfloat16 on the way count: a program that leaves them out, or rounds other values in their place, can miss the bound.
Values may be sent and summed in bfloat16 or wider, within the bound.
No kernel may reach another device: no remote copies, remote signals or barrier semaphores. Data moves between devices by JAX's collectives and lax.ppermute only.
A program may use at most 64 MiB of HBM per device.

v0:
```python
import math

import jax
import jax.numpy as jnp
from jax import lax
from jax.sharding import PartitionSpec as P

norm_eps = 1e-06
masked_score = -1e30


def attend(queries, key_rows, value_rows):
    scores = jnp.dot(queries, key_rows.T, preferred_element_type=jnp.float32) * queries.shape[
        -1
    ] ** (-0.5)
    row_top = jnp.max(scores, axis=-1, keepdims=True)
    lifted = jnp.exp(scores - row_top)
    weights = (lifted / jnp.sum(lifted, axis=-1, keepdims=True)).astype(jnp.bfloat16)
    return jnp.dot(weights, value_rows, preferred_element_type=jnp.float32).astype(jnp.bfloat16)


def normalize(totals, square_sums, width):
    return (totals * lax.rsqrt(square_sums / width + norm_eps)[:, None]).astype(jnp.bfloat16)


def combine_rows(partial_kv, squares, full_width):
    total_kv, total_squares = lax.psum((partial_kv, squares), "seq")
    return normalize(total_kv, total_squares, full_width)


def project_rows(caption_rows, caption_gain, weight_rows):
    videos, caption_len, feature_count = caption_rows.shape
    widened = caption_rows.astype(jnp.float32).reshape(videos * caption_len, feature_count)
    squares = jnp.sum(widened * widened, axis=-1)
    scaled = (widened * caption_gain).astype(jnp.bfloat16)
    partial_kv = jnp.dot(
        scaled, weight_rows.reshape(feature_count, -1), preferred_element_type=jnp.float32
    )
    return (partial_kv, squares)


def body(video_qkv, cross_query, captions, caption_gain, key_value_weight, caption_lengths):
    videos, local_heads, local_len, slots, head_size = video_qkv.shape
    work_items = video_qkv.reshape(videos * local_heads, local_len, slots, head_size)
    spread = lax.all_to_all(work_items, "seq", split_axis=0, concat_axis=1, tiled=True)
    full_len = spread.shape[1]
    block_len = math.gcd(full_len, 512)

    def self_item(one_item):
        blocks = one_item[:, 0].reshape(full_len // block_len, block_len, head_size)

        def one_block(block_rows):
            return attend(block_rows, one_item[:, 1], one_item[:, 2])

        return lax.map(one_block, blocks).reshape(full_len, head_size)

    attended = lax.map(self_item, spread)
    returned = lax.all_to_all(attended, "seq", split_axis=1, concat_axis=0, tiled=True)
    self_out = returned.reshape(videos, local_heads, local_len, head_size)
    feature_count = captions.shape[2]
    full_width = feature_count * lax.axis_size("seq")
    all_heads = key_value_weight.shape[2]
    caption_len = captions.shape[1]
    partial_kv, squares = project_rows(captions, caption_gain, key_value_weight)
    caption_kv = combine_rows(partial_kv, squares, full_width)
    caption_kv = caption_kv.reshape(videos, caption_len, 2, all_heads, head_size)
    caption_kv = lax.all_to_all(caption_kv, "tp", split_axis=3, concat_axis=1, tiled=True)
    scores = jnp.einsum(
        "vhqd,vkhd->vhqk", cross_query, caption_kv[:, :, 0], preferred_element_type=jnp.float32
    ) * head_size ** (-0.5)
    positions = jnp.arange(caption_kv.shape[1], dtype=jnp.int32)
    allowed = positions[None, :] < caption_lengths[:, None]
    scores = jnp.where(allowed[:, None, None, :], scores, masked_score)
    row_top = jnp.max(scores, axis=-1, keepdims=True)
    lifted = jnp.exp(scores - row_top)
    weights = (lifted / jnp.sum(lifted, axis=-1, keepdims=True)).astype(jnp.bfloat16)
    cross_out = jnp.einsum(
        "vhqk,vkhd->vhqd", weights, caption_kv[:, :, 1], preferred_element_type=jnp.float32
    ).astype(jnp.bfloat16)
    return (self_out, cross_out)


def solution(mesh):
    placed = (
        P(None, "tp", "seq", None, None),
        P(None, "tp", "seq", None),
        P(None, "tp", "seq"),
        P("seq"),
        P("seq", None, None, None),
        P(),
    )
    return jax.shard_map(
        body,
        mesh=mesh,
        in_specs=placed,
        out_specs=(P(None, "tp", "seq", None), P(None, "tp", "seq", None)),
        check_vma=False,
    )
```

profile of v0, /device:TPU:1, one launch (start us, length us, event | category | flops | bytes accessed | tf_op | source)
XLA Modules:
  0.0 622.0 jit_solution(10185909923213336736)
XLA Ops:
  7.2 0.0 copy-start
  7.2 0.0 copy-start.2
  7.2 0.0 copy-start.3
  7.2 0.0 copy-start.1
  7.2 14.9 %all-to-all-start = ((bf16[32,64,3,128]{3,1,2,0:T(8,128)(2,1)}), bf16[32,64,3,128]{3,1,2,0:T(8,128)(2,1)}, u32[]{:S(2)}, u32[]{:S(2)}) async-start(bf16[32,64,3,128]{3,1,2,0:T(8,128)(2,1)} %bitcast.78), calls=%async_computation | async-start | bytes 3145728 | tf_op jit(solution)/shard_map/all_to_all | solution.py:45
  22.1 0.0 all-reduce.2.cloned.1.call-start
  22.1 0.0 copy-done.2
  22.2 0.0 copy-done.3
  22.2 0.1 fusion.30
  22.3 0.0 copy-done.1
  22.3 4.4 fusion.16
  26.7 0.0 all-reduce.2.cloned.1.call-update
  26.8 24.2 %all-to-all-done = bf16[32,64,3,128]{3,1,2,0:T(8,128)(2,1)} async-done(((bf16[32,64,3,128]{3,1,2,0:T(8,128)(2,1)}), bf16[32,64,3,128]{3,1,2,0:T(8,128)(2,1)}, u32[]{:S(2)}, u32[]{:S(2)}) %all-to-all-start) | async-done | bytes 1572896 | tf_op jit(solution)/shard_map/all_to_all | solution.py:45
  50.9 1.6 copy.15
  52.6 10.9 %while.17 = (s32[]{:T(128)}, bf16[4,512,128]{2,1,0:T(8,128)(2,1)S(1)}, bf16[4,512,128]{2,1,0:T(8,128)(2,1)S(1)}, bf16[2048,3,128]{2,0,1:T(8,128)(2,1)S(1)}, s32[]{:T(128)}) while((s32[]{:T(128)}, bf16[4,512,128]{2,1,0:T(8,128)(2,1)S(1)}, bf16[4,512,128]{2,1,0:T(8,128)(2,1)S(1)}, bf16[2048,3,128]{2,0,1:T(8,128)(2,1)S(1)}, s32[]{:T(128)}) %tuple.35), condition=%wide.region_3.0_spmd, body=%wide.region_0.3_spmd.sunk | while | flops 546372608 | bytes 13903941 | solution.py:55
  52.7 0.8 multiply_reduce_fusion.2
  53.5 0.8 fusion.40
  54.4 1.1 fusion.41
  55.4 0.8 multiply_reduce_fusion.2
  56.2 0.8 fusion.40
  57.0 1.1 fusion.41
  58.1 0.8 multiply_reduce_fusion.2
  58.9 0.8 fusion.40
  59.7 1.1 fusion.41
  60.8 0.8 multiply_reduce_fusion.2
  61.6 0.8 fusion.40
  62.4 1.1 fusion.41
  63.4 8.1 %copy.27 = bf16[1,2048,128]{2,0,1:T(2,128)(2,1)S(1)} copy(bf16[1,2048,128]{2,1,0:T(8,128)(2,1)S(1)} %bitcast.80) | data formatting | bytes 1048576 | tf_op jit(solution)/shard_map/while/body/jit(dynamic_update_index_in_dim)/broadcast_in_dim | solution.py:57
  71.6 0.5 broadcast.43
  72.1 11.5 %reduce.1 = bf16[2048,128]{1,0:T(8,128)(2,1)S(1)} reduce(bf16[2048,1,128]{2,1,0:T(2,128)(2,1)S(1)} %bitcast.75, bf16[]{:T(256)} %broadcast.43), dimensions={1}, to_apply=%bitcast.60.reduce_sub_computation | reduce | bytes 1048578
  83.6 0.9 reshape.62
  84.6 7.6 %all-to-all-start.1 = ((bf16[32,2,4096]{2,1,0:T(2,128)(2,1)}), bf16[32,2,4096]{2,1,0:T(2,128)(2,1)S(1)}, u32[]{:S(2)}, u32[]{:S(2)}) async-start(bf16[32,2,4096]{2,1,0:T(2,128)(2,1)} %reshape.62), calls=%async_computation.1 | async-start | bytes 1048576 | tf_op jit(solution)/shard_map/all_to_all | solution.py:58
  92.2 0.1 reduce_sum.30
  92.3 110.0 %psum.15 = f32[192]{0:T(256)S(1)} all-reduce(f32[192]{0:T(256)S(1)} %reduce_sum.30), channel_id=1, replica_groups=mesh['seq'=32,'tp'=8] {'seq'}, use_global_device_ids=true, to_apply=%region_6.7 | all-reduce | flops 192 | bytes 1536 | tf_op jit(solution)/shard_map/psum | solution.py:27
  202.3 300.1 %all-reduce.2.cloned.1.call-done = f32[192,8192]{1,0:T(8,128)} async-done(((f32[192,8192]{1,0:T(8,128)}), f32[192,8192]{1,0:T(8,128)}) %all-reduce.2.cloned.1.call-update) | async-done | bytes 6291472 | tf_op jit(solution)/shard_map/psum | solution.py:27
  502.4 3.6 fusion.15
  506.0 0.9 copy.21
  506.9 5.0 copy.17
  511.9 0.0 all-to-all-done.1
  511.9 25.4 %all-to-all-start.2 = ((bf16[8,24,2,32,128]{4,2,1,0,3:T(2,128)(2,1)}), bf16[8,24,2,32,128]{4,2,1,0,3:T(2,128)(2,1)}, u32[]{:S(2)}, u32[]{:S(2)}) async-start(bf16[8,24,2,32,128]{4,2,1,0,3:T(2,128)(2,1)} %copy.17), calls=%async_computation.2 | async-start | bytes 6291456 | tf_op jit(solution)/shard_map/all_to_all | solution.py:67
  537.3 0.1 iota_compare_fusion
  537.3 0.5 reshape.63
  537.9 0.9 copy.19
  538.7 69.3 %all-to-all-done.2 = bf16[8,24,2,32,128]{4,2,1,0,3:T(2,128)(2,1)} async-done(((bf16[8,24,2,32,128]{4,2,1,0,3:T(2,128)(2,1)}), bf16[8,24,2,32,128]{4,2,1,0,3:T(2,128)(2,1)}, u32[]{:S(2)}, u32[]{:S(2)}) %all-to-all-start.2) | async-done | bytes 3145760 | tf_op jit(solution)/shard_map/all_to_all | solution.py:67
  608.0 2.7 copy.18
  610.7 1.1 fusion.24
  611.9 1.7 fusion.33
  613.5 1.6 fusion.25
  (6 shorter events, 0.1 us)
Async XLA Ops:
  7.2 603.6 %copy-start = (bf16[8,4,64,128]{3,2,1,0:T(8,128)(2,1)S(1)}, bf16[8,4,64,128]{3,2,1,0:T(8,128)(2,1)}, u32[]{:S(2)}) copy-start(bf16[8,4,64,128]{3,2,1,0:T(8,128)(2,1)} %param.9) | copy-start | bytes 1572868
  7.2 15.0 %copy-start.2 = (bf16[8,24,128]{2,1,0:T(8,128)(2,1)S(1)}, bf16[8,24,128]{2,1,0:T(8,128)(2,1)}, u32[]{:S(2)}) copy-start(bf16[8,24,128]{2,1,0:T(8,128)(2,1)} %param.10) | copy-start | bytes 147460
  7.2 15.0 %copy-start.3 = (f32[128]{0:T(128)S(1)}, f32[128]{0:T(128)}, u32[]{:S(2)}) copy-start(f32[128]{0:T(128)} %param.11) | copy-start | bytes 1540
  7.2 15.1 %copy-start.1 = (bf16[128,2,32,128]{3,2,1,0:T(8,128)(2,1)S(1)}, bf16[128,2,32,128]{3,2,1,0:T(8,128)(2,1)}, u32[]{:S(2)}) copy-start(bf16[128,2,32,128]{3,2,1,0:T(8,128)(2,1)} %param.12) | copy-start | bytes 6291460
  7.2 43.7 %all-to-all-start = ((bf16[32,64,3,128]{3,1,2,0:T(8,128)(2,1)}), bf16[32,64,3,128]{3,1,2,0:T(8,128)(2,1)}, u32[]{:S(2)}, u32[]{:S(2)}) async-start(bf16[32,64,3,128]{3,1,2,0:T(8,128)(2,1)} %bitcast.78), calls=%async_computation | async-start | bytes 3145728 | tf_op jit(solution)/shard_map/all_to_all | solution.py:45
  22.1 480.3 %all-reduce.2.cloned.1.call-start = ((), (), s32[]{:S(2)}) async-start(), calls=%async_computation.3 | async-start | bytes 12582912 | tf_op jit(solution)/shard_map/psum | solution.py:27
  84.6 427.3 %all-to-all-start.1 = ((bf16[32,2,4096]{2,1,0:T(2,128)(2,1)}), bf16[32,2,4096]{2,1,0:T(2,128)(2,1)S(1)}, u32[]{:S(2)}, u32[]{:S(2)}) async-start(bf16[32,2,4096]{2,1,0:T(2,128)(2,1)} %reshape.62), calls=%async_computation.1 | async-start | bytes 1048576 | tf_op jit(solution)/shard_map/all_to_all | solution.py:58
  511.9 25.4 %copy-start.4 = (s32[8]{0:T(128)S(1)}, s32[8]{0:T(128)}, u32[]{:S(2)}) copy-start(s32[8]{0:T(128)} %param.13) | copy-start | bytes 100
  511.9 96.2 %all-to-all-start.2 = ((bf16[8,24,2,32,128]{4,2,1,0,3:T(2,128)(2,1)}), bf16[8,24,2,32,128]{4,2,1,0,3:T(2,128)(2,1)}, u32[]{:S(2)}, u32[]{:S(2)}) async-start(bf16[8,24,2,32,128]{4,2,1,0,3:T(2,128)(2,1)} %copy.17), calls=%async_computation.2 | async-start | bytes 6291456 | tf_op jit(solution)/shard_map/all_to_all | solution.py:67
Sparse Core Ops, SparseCore 0:
  26.9 475.4 all-reduce.1
where the time goes:
time: 622 us
  waiting for transfers between devices  394 us (63%)
  blocking collectives  110 us (18%)
  starting transfers between devices  47.9 us (8%)
  local copies, waits for them, and re-layouts  21.2 us (3%)
  other arithmetic  20.3 us (3%)
  matrix products  14.5 us (2%)
  between operations  14.2 us (2%)
    psum x1, waiting for transfers between devices, combine_rows(): total_kv, total_squares = lax.psum((partial_kv, squares), 'seq')  300 us
    psum x1, blocking collectives, combine_rows(): total_kv, total_squares = lax.psum((partial_kv, squares), 'seq')  110 us
    all_to_all x1, waiting for transfers between devices, body(): lax.all_to_all(caption_kv, 'tp', split_axis=3, concat_axis=1, tiled=True)  69.3 us
    all_to_all x1, starting transfers between devices, body(): lax.all_to_all(caption_kv, 'tp', split_axis=3, concat_axis=1, tiled=True)  25.4 us
    all_to_all x1, waiting for transfers between devices, body(): lax.all_to_all(work_items, 'seq', split_axis=0, concat_axis=1, tiled=True)  24.2 us
    unnamed x2, other arithmetic  15.2 us
    all_to_all x1, starting transfers between devices, body(): lax.all_to_all(work_items, 'seq', split_axis=0, concat_axis=1, tiled=True)  14.9 us
  transfers between devices with their start and end apart: 4, of which 3 were waited for; matrix products, arithmetic and copies ran while one was open for 8% of the time, Pallas kernels for 0%

commit v1 on v0

v1 whole, which is shorter than its diff:
```python
import jax
import jax.numpy as jnp
from jax import lax
from jax.experimental import pallas as pl
from jax.experimental.pallas import tpu as pltpu
from jax.sharding import Mesh
from jax.sharding import PartitionSpec as P

norm_eps = 1e-06
masked_score = -1e30
log2e = 1.4426950408889634
AXES = ("y", "zh", "x", "zl", "c")
SEQ = ("y", "zh", "x")
XY = ("y", "x")
TP = ("zl", "c")
SWAP = [(0, 1), (1, 0)]
VMEM_LIMIT = 40 * 1024 * 1024


def nt_dot(a, b):
    return lax.dot_general(a, b, (((1,), (1,)), ((), ())), preferred_element_type=jnp.float32)


def softmax_dot(scores, values, scale):
    top = jnp.max(scores, axis=-1, keepdims=True)
    lifted = jnp.exp2((scores - top) * (scale * log2e))
    total = jnp.sum(lifted, axis=-1, keepdims=True)
    out = jnp.dot(lifted.astype(jnp.bfloat16), values, preferred_element_type=jnp.float32)
    return (out / total).astype(jnp.bfloat16)


def self_kernel(q_ref, kv_ref, o_ref):
    head_size = o_ref.shape[-1]
    scores = nt_dot(q_ref[:, :head_size], kv_ref[:, head_size : 2 * head_size])
    o_ref[...] = softmax_dot(scores, kv_ref[:, 2 * head_size :], head_size ** (-0.5))


def self_attention(item, block=256):
    full_len, width = item.shape
    head_size = width // 3
    return pl.pallas_call(
        self_kernel,
        out_shape=jax.ShapeDtypeStruct((full_len, head_size), item.dtype),
        grid=(full_len // block,),
        in_specs=[
            pl.BlockSpec((block, width), lambda i: (i, 0)),
            pl.BlockSpec((full_len, width), lambda i: (0, 0)),
        ],
        out_specs=pl.BlockSpec((block, head_size), lambda i: (i, 0)),
        compiler_params=pltpu.CompilerParams(vmem_limit_bytes=VMEM_LIMIT),
        cost_estimate=pl.CostEstimate(
            flops=4 * full_len * full_len * head_size,
            bytes_accessed=8 * full_len * head_size,
            transcendentals=full_len * full_len,
        ),
        name="self_attention",
    )(item, item)


def project_kernel(mine_ref, other_ref, w_ref, part_ref, sq_ref):
    z_count, sources, rows, feats = mine_ref.shape
    half = z_count * rows
    for which, ref in enumerate((mine_ref, other_ref)):
        squares = jnp.zeros((half, 1), jnp.float32)
        total = jnp.zeros((half, part_ref.shape[1]), jnp.float32)
        for s in range(sources):
            block = ref[:, s].astype(jnp.float32).reshape(half, feats)
            squares += jnp.sum(block * block, axis=-1, keepdims=True)
            gains = w_ref[s, feats : feats + 16, :feats].astype(jnp.float32)
            gain = gains[0:1] + gains[1:2] + gains[2:3]
            scaled = (block * gain).astype(jnp.bfloat16)
            total += jnp.dot(scaled, w_ref[s, :feats], preferred_element_type=jnp.float32)
        part_ref[which * half : (which + 1) * half] = total
        spread = jnp.broadcast_to(squares, (half, 128))
        sq_ref[which] = spread.T[:8]


def project(mine, other, weights):
    z_count, sources, rows, feats = mine.shape
    half = z_count * rows
    return pl.pallas_call(
        project_kernel,
        out_shape=(
            jax.ShapeDtypeStruct((2 * half, weights.shape[-1]), jnp.float32),
            jax.ShapeDtypeStruct((2, 8, half), jnp.float32),
        ),
        compiler_params=pltpu.CompilerParams(vmem_limit_bytes=VMEM_LIMIT),
        cost_estimate=pl.CostEstimate(
            flops=4 * half * sources * feats * weights.shape[-1],
            bytes_accessed=4 * half * sources * feats,
            transcendentals=0,
        ),
        name="project",
    )(mine, other, weights)


def cross_kernel(full_width, q_ref, part_a, part_b, sq_a, sq_b, allowed_ref, o_ref):
    sources, videos, local_len, head_size = q_ref.shape
    half = sq_a.shape[-1]
    blocks, rows = 8, part_a.shape[0] // 8
    per = rows // videos
    inverse = []
    for which in range(2):
        squares = sq_a[which, 0:1] + sq_b[which, 0:1]
        inv = lax.rsqrt(squares / full_width + norm_eps)
        inverse.append(jnp.broadcast_to(inv, (128, half)).T)
    kv = []
    for b in range(blocks):
        span = slice(b * rows, (b + 1) * rows)
        total = part_a[span] + part_b[span]
        at = (b % 4) * rows
        inv = inverse[b // 4][at : at + rows]
        kv.append(jnp.concatenate([total[:, :head_size] * inv, total[:, head_size:] * inv], axis=1))
    for v in range(videos):
        this = jnp.concatenate([blk[v * per : (v + 1) * per] for blk in kv], axis=0)
        this = this.astype(jnp.bfloat16)
        queries = q_ref[:, v].reshape(sources * local_len, head_size)
        scores = nt_dot(queries, this[:, :head_size])
        scores = jnp.where(allowed_ref[v, 0:1] > 0, scores, masked_score)
        out = softmax_dot(scores, this[:, head_size:], head_size ** (-0.5))
        o_ref[:, v] = out.reshape(sources, local_len, head_size)


def cross_attention(queries, part_a, part_b, sq_a, sq_b, allowed, full_width):
    sources, videos, local_len, head_size = queries.shape
    count = sources * videos * local_len * allowed.shape[-1]

    def kernel(*refs):
        cross_kernel(full_width, *refs)

    return pl.pallas_call(
        kernel,
        out_shape=jax.ShapeDtypeStruct(queries.shape, queries.dtype),
        compiler_params=pltpu.CompilerParams(vmem_limit_bytes=VMEM_LIMIT),
        cost_estimate=pl.CostEstimate(
            flops=4 * count * head_size,
            bytes_accessed=4 * sources * videos * local_len * head_size,
            transcendentals=count,
        ),
        name="cross_attention",
    )(queries, part_a, part_b, sq_a, sq_b, allowed)


def three_parts(values):
    high = lax.reduce_precision(values, 8, 7)
    rest = values - high
    middle = lax.reduce_precision(rest, 8, 7)
    return [p.astype(jnp.bfloat16) for p in (high, middle, rest - middle)]


def body(video_qkv, cross_query, captions, caption_gain, key_value_weight, caption_lengths):
    videos, local_heads, local_len, slots, head_size = video_qkv.shape
    caption_len, feats = captions.shape[1:]
    ny, nx, nz = lax.axis_size("y"), lax.axis_size("x"), lax.axis_size("zl")
    pair = videos // ny
    group = ny * nx
    tp = lax.axis_index("zl") * 2 + lax.axis_index("c")
    full_width = feats * group * 2

    rows = captions.reshape(ny, 1, pair * caption_len, feats)
    rows = jnp.broadcast_to(rows, (ny, nx, pair * caption_len, feats))
    rows = rows.reshape(group, pair * caption_len, feats)
    rows = lax.all_to_all(rows, XY, split_axis=0, concat_axis=0, tiled=True)
    rows = lax.all_gather(rows, "zl", axis=0, tiled=False)
    other_rows = lax.ppermute(rows, "c", SWAP)

    weights = lax.dynamic_slice_in_dim(key_value_weight, tp * local_heads, local_heads, axis=2)
    weights = weights.transpose(2, 0, 1, 3).reshape(local_heads, feats, 2 * head_size)
    gains = jnp.stack(three_parts(caption_gain))
    gains = jnp.pad(gains, ((0, 13), (0, 2 * head_size - feats)))
    gains = jnp.broadcast_to(gains, (local_heads,) + gains.shape)
    weights = jnp.concatenate([weights, gains], axis=1)
    weights = jnp.broadcast_to(weights, (ny,) + weights.shape).reshape(
        (group,) + weights.shape[1:]
    )
    weights = lax.all_to_all(weights, XY, split_axis=0, concat_axis=0, tiled=True)

    items = video_qkv.reshape(videos * local_heads, local_len, slots * head_size)
    items = lax.all_to_all(items, SEQ, split_axis=0, concat_axis=0, tiled=True)

    queries = cross_query.reshape(ny, pair, nx, local_len, head_size).transpose(0, 2, 1, 3, 4)
    queries = queries.reshape(group, pair, local_len, head_size)
    queries = lax.all_to_all(queries, XY, split_axis=0, concat_axis=0, tiled=True)

    part, squares = project(rows, other_rows, weights)
    far_part = lax.ppermute(part, "zh", SWAP)
    far_squares = lax.ppermute(squares, "zh", SWAP)

    attended = self_attention(items.reshape(-1, slots * head_size))
    attended = attended.reshape(videos * local_heads, local_len, head_size)
    self_out = lax.all_to_all(attended, SEQ, split_axis=0, concat_axis=0, tiled=True)
    self_out = self_out.reshape(videos, local_heads, local_len, head_size)

    core = lax.axis_index("c")
    which, z, token = jnp.meshgrid(
        jnp.arange(2), jnp.arange(nz), jnp.arange(caption_len), indexing="ij"
    )
    cores = jnp.where(which == 0, core, 1 - core)
    positions = ((z * 2 + cores) * caption_len + token).reshape(-1)
    lengths = lax.dynamic_slice_in_dim(caption_lengths, lax.axis_index("y") * pair, pair)
    allowed = (positions[None, :] < lengths[:, None]).astype(jnp.float32)
    allowed = jnp.broadcast_to(allowed[:, None, :], (pair, 8, allowed.shape[-1]))

    crossed = cross_attention(queries, part, far_part, squares, far_squares, allowed, full_width)
    crossed = lax.all_to_all(crossed, XY, split_axis=0, concat_axis=0, tiled=True)
    crossed = crossed.reshape(ny, nx, pair, local_len, head_size).transpose(0, 2, 1, 3, 4)
    cross_out = crossed.reshape(videos, local_heads, local_len, head_size)
    return (self_out, cross_out)


def solution(mesh):
    devices = mesh.devices.reshape(4, 2, 4, 4, 2)
    placed = (
        P(None, TP, SEQ, None, None),
        P(None, TP, SEQ, None),
        P(None, TP, SEQ),
        P(SEQ),
        P(SEQ, None, None, None),
        P(),
    )
    return jax.shard_map(
        body,
        mesh=Mesh(devices, AXES),
        in_specs=placed,
        out_specs=(P(None, TP, SEQ, None), P(None, TP, SEQ, None)),
        check_vma=False,
    )
```

time: 622 us -> 195 us (0.31)
  the two profiles are of different devices: /device:TPU:1 before, /device:TPU:66 now
where the time goes in v1:
time: 195 us; the launch traced here: 194 us
  waiting for transfers between devices  58.5 us (30%)
  starting transfers between devices  51.5 us (26%)
  blocking collectives  47.7 us (24%)
  local copies, waits for them, and re-layouts  18.4 us (9%)
  Pallas kernels  16.8 us (9%)
    all_gather x1, blocking collectives, body(): rows = lax.all_gather(rows, 'zl', axis=0, tiled=False)  47.7 us
    ppermute x1, waiting for transfers between devices, body(): far_squares = lax.ppermute(squares, 'zh', SWAP)  18.3 us
    all_to_all x1, waiting for transfers between devices, body(): lax.all_to_all(attended, SEQ, split_axis=0, concat_axis=0, tiled=True)  17.9 us
    all_to_all x1, starting transfers between devices, body(): lax.all_to_all(attended, SEQ, split_axis=0, concat_axis=0, tiled=True)  11.6 us
    pallas_call x1, Pallas kernels, self_attention(): pl.pallas_call(self_kernel, out_shape=jax.ShapeDtypeStruct((full_len, hea...  10.7 us
    all_to_all x1, starting transfers between devices, body(): items = lax.all_to_all(items, SEQ, split_axis=0, concat_axis=0, tiled=True)  9.39 us
    all_to_all x1, waiting for transfers between devices, body(): lax.all_to_all(queries, XY, split_axis=0, concat_axis=0, tiled=True)  8.19 us
    all_to_all x1, starting transfers between devices, body(): rows = lax.all_to_all(rows, XY, split_axis=0, concat_axis=0, tiled=True)  7.48 us
  transfers between devices with their start and end apart: 9, of which 6 were waited for; matrix products, arithmetic and copies ran while one was open for 7% of the time, Pallas kernels for 9%

profile of v1, /device:TPU:66, one launch (start us, length us, event | category | flops | bytes accessed | tf_op | source)
XLA Modules:
  0.0 194.0 jit_solution(13058628074283083856)
XLA Ops:
  0.6 0.0 copy-start
  0.6 1.6 broadcast_in_dim.38
  2.3 7.5 %all-to-all-start.3 = ((bf16[16,48,128]{2,1,0:T(8,128)(2,1)}), bf16[16,48,128]{2,1,0:T(8,128)(2,1)S(1)}, u32[]{:S(2)}, u32[]{:S(2)}) async-start(bf16[16,48,128]{2,1,0:T(8,128)(2,1)} %bitcast.7), calls=%async_computation.3 | async-start | bytes 393216 | tf_op jit(solution)/shard_map/all_to_all | solution.py:163
  9.8 1.9 copy.17
  11.7 5.1 %all-to-all-done.3 = bf16[16,48,128]{2,1,0:T(8,128)(2,1)S(1)} async-done(((bf16[16,48,128]{2,1,0:T(8,128)(2,1)}), bf16[16,48,128]{2,1,0:T(8,128)(2,1)S(1)}, u32[]{:S(2)}, u32[]{:S(2)}) %all-to-all-start.3) | async-done | bytes 196640 | tf_op jit(solution)/shard_map/all_to_all | solution.py:163
  16.8 0.0 copy-start.3
  16.8 0.7 copy-done.3
  17.4 4.8 %all-to-all-start.2 = ((bf16[16,2,64,128]{3,2,1,0:T(8,128)(2,1)}), bf16[16,2,64,128]{3,2,1,0:T(8,128)(2,1)S(1)}, u32[]{:S(2)}, u32[]{:S(2)}) async-start(bf16[16,2,64,128]{3,2,1,0:T(8,128)(2,1)} %bitcast.5), calls=%async_computation.2 | async-start | bytes 1048576 | tf_op jit(solution)/shard_map/all_to_all | solution.py:183
  22.3 0.0 copy-done
  22.3 0.1 constant_dynamic-slice_fusion
  22.4 0.2 copy.22
  22.6 0.0 copy-done.5
  22.7 0.1 copy.23
  22.9 0.1 pad_maximum_fusion
  23.0 0.2 copy.20
  23.2 8.2 %all-to-all-done.2.refs_0_ = bf16[16,2,64,128]{3,2,1,0:T(8,128)(2,1)S(1)} async-done(((bf16[16,2,64,128]{3,2,1,0:T(8,128)(2,1)}), bf16[16,2,64,128]{3,2,1,0:T(8,128)(2,1)S(1)}, u32[]{:S(2)}, u32[]{:S(2)}) %all-to-all-start.2) | async-done | bytes 524320 | tf_op jit(solution)/shard_map/all_to_all | solution.py:183
  31.4 0.0 copy-start.1
  31.4 1.2 broadcast_in_dim.40
  32.6 0.0 copy-done.1
  32.6 4.9 %all-to-all-start.4 = ((bf16[16,144,256]{2,1,0:T(8,128)(2,1)}), bf16[16,144,256]{2,1,0:T(8,128)(2,1)S(1)}, u32[]{:S(2)}, u32[]{:S(2)}) async-start(bf16[16,144,256]{2,1,0:T(8,128)(2,1)} %bitcast.24), calls=%async_computation.4 | async-start | bytes 2359296 | tf_op jit(solution)/shard_map/all_to_all | solution.py:176
  37.6 4.3 %copy.16 = bf16[8,4,64,3,128]{4,3,2,1,0:T(4,128)(2,1)} copy(bf16[8,4,64,3,128]{4,2,3,1,0:T(8,128)(2,1)} %param.6) | data formatting | bytes 3145728 | tf_op args[0]
  41.8 5.1 %reshape.92 = bf16[32,64,384]{2,1,0:T(8,128)(2,1)} reshape(bf16[8,4,64,3,128]{4,3,2,1,0:T(4,128)(2,1)} %copy.16) | data formatting | bytes 3145728 | tf_op jit(solution)/shard_map/reshape | solution.py:178
  46.9 6.4 %all-to-all-done.4.w_ref = bf16[16,144,256]{2,1,0:T(8,128)(2,1)S(1)} async-done(((bf16[16,144,256]{2,1,0:T(8,128)(2,1)}), bf16[16,144,256]{2,1,0:T(8,128)(2,1)S(1)}, u32[]{:S(2)}, u32[]{:S(2)}) %all-to-all-start.4) | async-done | bytes 1179680 | tf_op jit(solution)/shard_map/all_to_all | solution.py:176
  53.3 9.4 %all-to-all-start = ((bf16[32,64,384]{2,1,0:T(8,128)(2,1)}), bf16[32,64,384]{2,1,0:T(8,128)(2,1)}, u32[]{:S(2)}, u32[]{:S(2)}) async-start(bf16[32,64,384]{2,1,0:T(8,128)(2,1)} %reshape.92), calls=%async_computation | async-start | bytes 3145728 | tf_op jit(solution)/shard_map/all_to_all | solution.py:179
  62.7 0.0 copy-done.4
  62.7 47.7 %all-gather = bf16[64,48,128]{2,1,0:T(8,128)(2,1)} all-gather(bf16[16,48,128]{2,1,0:T(8,128)(2,1)S(1)} %copy-done.4), channel_id=2, replica_groups=mesh['y'=4,'zh'=2,'x'=4,'zl'=4,'c'=2] {'zl'}, dimensions={0}, use_global_device_ids=true | all-gather | bytes 983040 | tf_op jit(solution)/shard_map/all_gather | solution.py:164
  110.4 0.0 collective-permute-start
  110.4 2.6 %collective-permute-done.other_ref = bf16[4,16,48,128]{3,2,1,0:T(8,128)(2,1)} collective-permute-done((bf16[4,16,48,128]{3,2,1,0:T(8,128)(2,1)}, bf16[4,16,48,128]{3,2,1,0:T(8,128)(2,1)}, u32[]{:S(2)}, u32[]{:S(2)}) %collective-permute-start) | collective-permute-done | bytes 786464 | tf_op jit(solution)/shard_map/ppermute | solution.py:165
  113.0 3.1 %project.1 = (f32[384,256]{1,0:T(8,128)}, f32[2,8,192]{2,1,0:T(8,128)S(1)}) custom-call(bf16[4,16,48,128]{3,2,1,0:T(8,128)(2,1)} %bitcast.8.mine_ref, bf16[4,16,48,128]{3,2,1,0:T(8,128)(2,1)} %collective-permute-done.other_ref, bf16[16,144,256]{2,1,0:T(8,128)(2,1)S(1)} %all-to-all-done.4.w_ref), custom_call_target="tpu_custom_call" | custom-call | flops 402653184 | bytes 1572864 | tf_op jit(solution)/shard_map/project/pallas_call | solution.py:81
  116.1 4.9 %collective-permute-start.1 = (f32[384,256]{1,0:T(8,128)}, f32[384,256]{1,0:T(8,128)S(1)}, u32[]{:S(2)}, u32[]{:S(2)}) collective-permute-start(f32[384,256]{1,0:T(8,128)} %get-tuple-element.4.refs_1_), channel_id=1, source_target_pairs={{0,32},{32,0},{1,33},{33,1},{2,34},{34,2},{3,35},{35,3},{4,36},{36... | collective-permute-start | bytes 1179656 | tf_op jit(solution)/shard_map/ppermute | solution.py:186
  121.0 0.1 iota_add_fusion
  121.1 0.1 add.33
  121.2 0.0 copy-done.6
  121.2 0.1 dynamic_slice.7
  121.2 1.1 collective-permute-start.2
  122.3 0.1 compare_convert_fusion
  122.4 18.3 %collective-permute-done.2.refs_4_ = f32[2,8,192]{2,1,0:T(8,128)S(1)} collective-permute-done((f32[2,8,192]{2,1,0:T(8,128)S(1)}, f32[2,8,192]{2,1,0:T(8,128)S(1)}, u32[]{:S(2)}, u32[]{:S(2)}) %collective-permute-start.2) | collective-permute-done | bytes 12320 | tf_op jit(solution)/shard_map/ppermute | solution.py:187
  140.7 0.0 collective-permute-done.1.refs_2_
  140.7 1.0 copy-done.2
  141.7 3.0 %cross_attention.1 = bf16[16,2,64,128]{3,2,1,0:T(8,128)(2,1)} custom-call(bf16[16,2,64,128]{3,2,1,0:T(8,128)(2,1)S(1)} %copy-done.2, f32[384,256]{1,0:T(8,128)} %get-tuple-element.4.refs_1_, f32[384,256]{1,0:T(8,128)S(1)} %collective-permute-done.1.refs_2_, f32[2,8,192]{2,1,0:T(8,128)S(1)} %get-tuple-element.5.refs_3_, ...), custom_call_target="tpu_custom_call" | custom-call | flops 201326592 | bytes 1048576 | tf_op jit(solution)/shard_map/cross_attention/pallas_call | solution.py:131
  144.7 0.0 all-to-all-done
  144.7 7.4 %all-to-all-start.5 = ((bf16[16,2,64,128]{3,2,1,0:T(8,128)(2,1)}), bf16[16,2,64,128]{3,2,1,0:T(8,128)(2,1)S(1)}, u32[]{:S(2)}, u32[]{:S(2)}) async-start(bf16[16,2,64,128]{3,2,1,0:T(8,128)(2,1)} %cross_attention.1), calls=%async_computation.5 | async-start | bytes 1048576 | tf_op jit(solution)/shard_map/all_to_all | solution.py:205
  152.1 10.7 %self_attention.1 = bf16[2048,128]{1,0:T(8,128)(2,1)} custom-call(bf16[2048,384]{1,0:T(8,128)(2,1)} %bitcast.q_ref.kv_ref, bf16[2048,384]{1,0:T(8,128)(2,1)} %bitcast.q_ref.kv_ref), custom_call_target="tpu_custom_call" | custom-call | flops 2147483648 | bytes 2097152 | tf_op jit(solution)/shard_map/self_attention/pallas_call | solution.py:41
  162.8 0.0 all-to-all-done.5
  162.8 11.6 %all-to-all-start.1 = ((bf16[32,64,128]{2,1,0:T(8,128)(2,1)}), bf16[32,64,128]{2,1,0:T(8,128)(2,1)S(1)}, u32[]{:S(2)}, u32[]{:S(2)}) async-start(bf16[32,64,128]{2,1,0:T(8,128)(2,1)} %bitcast.1), calls=%async_computation.1 | async-start | bytes 1048576 | tf_op jit(solution)/shard_map/all_to_all | solution.py:191
  174.4 0.8 copy.21
  175.3 17.9 %all-to-all-done.1 = bf16[32,64,128]{2,1,0:T(8,128)(2,1)S(1)} async-done(((bf16[32,64,128]{2,1,0:T(8,128)(2,1)}), bf16[32,64,128]{2,1,0:T(8,128)(2,1)S(1)}, u32[]{:S(2)}, u32[]{:S(2)}) %all-to-all-start.1) | async-done | bytes 524320 | tf_op jit(solution)/shard_map/all_to_all | solution.py:191
  193.2 0.8 copy.25
  (11 shorter events, 0.1 us)
Async XLA Ops:
  0.6 21.6 %copy-start = (bf16[128,2,32,128]{3,2,1,0:T(8,128)(2,1)S(1)}, bf16[128,2,32,128]{3,2,1,0:T(8,128)(2,1)}, u32[]{:S(2)}) copy-start(bf16[128,2,32,128]{3,2,1,0:T(8,128)(2,1)} %param.10) | copy-start | bytes 6291460
  2.3 14.5 %all-to-all-start.3 = ((bf16[16,48,128]{2,1,0:T(8,128)(2,1)}), bf16[16,48,128]{2,1,0:T(8,128)(2,1)S(1)}, u32[]{:S(2)}, u32[]{:S(2)}) async-start(bf16[16,48,128]{2,1,0:T(8,128)(2,1)} %bitcast.7), calls=%async_computation.3 | async-start | bytes 393216 | tf_op jit(solution)/shard_map/all_to_all | solution.py:163
  9.8 12.9 %copy-start.5 = (f32[128]{0:T(128)S(1)}, f32[128]{0:T(128)}, u32[]{:S(2)}) copy-start(f32[128]{0:T(128)} %param.9) | copy-start | bytes 1540
  16.8 0.7 copy-start.3
  17.4 14.0 %all-to-all-start.2 = ((bf16[16,2,64,128]{3,2,1,0:T(8,128)(2,1)}), bf16[16,2,64,128]{3,2,1,0:T(8,128)(2,1)S(1)}, u32[]{:S(2)}, u32[]{:S(2)}) async-start(bf16[16,2,64,128]{3,2,1,0:T(8,128)(2,1)} %bitcast.5), calls=%async_computation.2 | async-start | bytes 1048576 | tf_op jit(solution)/shard_map/all_to_all | solution.py:183
  31.4 1.2 copy-start.1
  32.6 20.7 %all-to-all-start.4 = ((bf16[16,144,256]{2,1,0:T(8,128)(2,1)}), bf16[16,144,256]{2,1,0:T(8,128)(2,1)S(1)}, u32[]{:S(2)}, u32[]{:S(2)}) async-start(bf16[16,144,256]{2,1,0:T(8,128)(2,1)} %bitcast.24), calls=%async_computation.4 | async-start | bytes 2359296 | tf_op jit(solution)/shard_map/all_to_all | solution.py:176
  46.9 15.8 %copy-start.4 = (bf16[16,48,128]{2,1,0:T(8,128)(2,1)S(1)}, bf16[16,48,128]{2,1,0:T(8,128)(2,1)}, u32[]{:S(2)}) copy-start(bf16[16,48,128]{2,1,0:T(8,128)(2,1)} %copy-done.3) | copy-start | bytes 589828
  53.3 91.4 %all-to-all-start = ((bf16[32,64,384]{2,1,0:T(8,128)(2,1)}), bf16[32,64,384]{2,1,0:T(8,128)(2,1)}, u32[]{:S(2)}, u32[]{:S(2)}) async-start(bf16[32,64,384]{2,1,0:T(8,128)(2,1)} %reshape.92), calls=%async_computation | async-start | bytes 3145728 | tf_op jit(solution)/shard_map/all_to_all | solution.py:179
  110.4 10.8 %copy-start.6 = (s32[8]{0:T(128)S(1)}, s32[8]{0:T(128)}, u32[]{:S(2)}) copy-start(s32[8]{0:T(128)} %param.11) | copy-start | bytes 100
  110.4 2.6 %collective-permute-start = (bf16[4,16,48,128]{3,2,1,0:T(8,128)(2,1)}, bf16[4,16,48,128]{3,2,1,0:T(8,128)(2,1)}, u32[]{:S(2)}, u32[]{:S(2)}) collective-permute-start(bf16[4,16,48,128]{3,2,1,0:T(8,128)(2,1)} %bitcast.8.mine_ref), channel_id=1, source_target_pairs={{0,1},{1,0},{2,3},{3,2},{4,5},{5,4},{6,7},{7,6},{8,9},{9,8},{10,11... | collective-permute-start | bytes 2359304 | tf_op jit(solution)/shard_map/ppermute | solution.py:165
  116.1 24.6 %collective-permute-start.1 = (f32[384,256]{1,0:T(8,128)}, f32[384,256]{1,0:T(8,128)S(1)}, u32[]{:S(2)}, u32[]{:S(2)}) collective-permute-start(f32[384,256]{1,0:T(8,128)} %get-tuple-element.4.refs_1_), channel_id=1, source_target_pairs={{0,32},{32,0},{1,33},{33,1},{2,34},{34,2},{3,35},{35,3},{4,36},{36... | collective-permute-start | bytes 1179656 | tf_op jit(solution)/shard_map/ppermute | solution.py:186
  121.2 19.4 %collective-permute-start.2 = (f32[2,8,192]{2,1,0:T(8,128)S(1)}, f32[2,8,192]{2,1,0:T(8,128)S(1)}, u32[]{:S(2)}, u32[]{:S(2)}) collective-permute-start(f32[2,8,192]{2,1,0:T(8,128)S(1)} %get-tuple-element.5.refs_3_), channel_id=1, source_target_pairs={{0,32},{32,0},{1,33},{33,1},{2,34},{34,2},{3,35},{35,3},{4,36},{36... | collective-permute-start | bytes 36872 | tf_op jit(solution)/shard_map/ppermute | solution.py:187
  140.7 1.0 copy-start.2
  144.7 18.1 %all-to-all-start.5 = ((bf16[16,2,64,128]{3,2,1,0:T(8,128)(2,1)}), bf16[16,2,64,128]{3,2,1,0:T(8,128)(2,1)S(1)}, u32[]{:S(2)}, u32[]{:S(2)}) async-start(bf16[16,2,64,128]{3,2,1,0:T(8,128)(2,1)} %cross_attention.1), calls=%async_computation.5 | async-start | bytes 1048576 | tf_op jit(solution)/shard_map/all_to_all | solution.py:205
  162.8 30.4 %all-to-all-start.1 = ((bf16[32,64,128]{2,1,0:T(8,128)(2,1)}), bf16[32,64,128]{2,1,0:T(8,128)(2,1)S(1)}, u32[]{:S(2)}, u32[]{:S(2)}) async-start(bf16[32,64,128]{2,1,0:T(8,128)(2,1)} %bitcast.1), calls=%async_computation.1 | async-start | bytes 1048576 | tf_op jit(solution)/shard_map/all_to_all | solution.py:191

commit v2 on v1

v2 whole, which is shorter than its diff:
```python
import jax
import jax.numpy as jnp
from jax import lax
from jax.experimental import pallas as pl
from jax.experimental.pallas import tpu as pltpu
from jax.sharding import Mesh
from jax.sharding import PartitionSpec as P

norm_eps = 1e-06
masked_score = -1e30
log2e = 1.4426950408889634
AXES = ("y", "zh", "x", "zl", "c")
SEQ = ("y", "zh", "x")
XY = ("y", "x")
TP = ("zl", "c")
SWAP = [(0, 1), (1, 0)]
PLACE_FLOPS = 100_000_000_000
VMEM_LIMIT = 40 * 1024 * 1024


def nt_dot(a, b):
    return lax.dot_general(a, b, (((1,), (1,)), ((), ())), preferred_element_type=jnp.float32)


def softmax_dot(scores, values, scale):
    top = jnp.max(scores, axis=-1, keepdims=True)
    lifted = jnp.exp2((scores - top) * (scale * log2e))
    total = jnp.sum(lifted, axis=-1, keepdims=True)
    out = jnp.dot(lifted.astype(jnp.bfloat16), values, preferred_element_type=jnp.float32)
    return (out / total).astype(jnp.bfloat16)


def params():
    return pltpu.CompilerParams(vmem_limit_bytes=VMEM_LIMIT)


def whole(array):
    return pl.BlockSpec(array.shape, lambda *_: (0,) * array.ndim)


def pick_kernel(zh_ref, x_ref, o_ref):
    o_ref[...] = x_ref[...].reshape(o_ref.shape)


def pick(zh, items):
    ny, _, nx, height, lanes = items.shape
    return pl.pallas_call(
        pick_kernel,
        out_shape=jax.ShapeDtypeStruct((ny * nx, height, lanes), items.dtype),
        grid_spec=pltpu.PrefetchScalarGridSpec(
            num_scalar_prefetch=1,
            grid=(2,),
            in_specs=[
                pl.BlockSpec(
                    (ny // 2, 1, nx, height, lanes), lambda i, zh_ref: (i, zh_ref[0], 0, 0, 0)
                )
            ],
            out_specs=pl.BlockSpec((ny // 2 * nx, height, lanes), lambda i, zh_ref: (i, 0, 0)),
        ),
        name="pick",
    )(zh, items)


def pack_kernel(zh_ref, x_ref, q_ref, *refs):
    o_ref = refs[-1]
    ny, _, nx, height, lanes = x_ref.shape
    pair, local_len = q_ref.shape[1], q_ref.shape[3]
    o_ref[:, :height] = x_ref[...].reshape(ny * nx, height, lanes)
    for y in range(ny):
        for j in range(pair):
            at = 2 * height + j * local_len
            o_ref[y * nx : (y + 1) * nx, at : at + local_len] = q_ref[y, j]


def pack(zh, items, queries, earlier):
    ny, _, nx, height, lanes = items.shape
    pair, local_len = queries.shape[1], queries.shape[3]
    total = 2 * height + pair * local_len
    return pl.pallas_call(
        pack_kernel,
        out_shape=jax.ShapeDtypeStruct((ny * nx, total, lanes), items.dtype),
        grid_spec=pltpu.PrefetchScalarGridSpec(
            num_scalar_prefetch=1,
            grid=(2,),
            in_specs=[
                pl.BlockSpec(
                    (ny // 2, 1, nx, height, lanes), lambda i, zh_ref: (i, zh_ref[0], 0, 0, 0)
                ),
                pl.BlockSpec(
                    (ny // 2, pair, nx, local_len, lanes), lambda i, zh_ref: (i, 0, 0, 0, 0)
                ),
            ]
            + [pl.BlockSpec(memory_space=pl.ANY)] * len(earlier),
            out_specs=pl.BlockSpec((ny // 2 * nx, total, lanes), lambda i, zh_ref: (i, 0, 0)),
        ),
        name="pack",
    )(zh, items, queries, *earlier)


def place_kernel(x_ref, _, o_ref):
    o_ref[...] = x_ref[...]


def place(buffer, part, at):
    count, height, lanes = part.shape
    return pl.pallas_call(
        place_kernel,
        out_shape=jax.ShapeDtypeStruct(buffer.shape, buffer.dtype),
        grid=(2,),
        in_specs=[
            pl.BlockSpec((count // 2, height, lanes), lambda i: (i, 0, 0)),
            pl.BlockSpec(memory_space=pl.ANY),
        ],
        out_specs=pl.BlockSpec((count // 2, height, lanes), lambda i: (i, at, 0)),
        input_output_aliases={1: 0},
        cost_estimate=pl.CostEstimate(
            flops=PLACE_FLOPS, bytes_accessed=4 * part.size, transcendentals=0
        ),
        name="place",
    )(part, buffer)


def take_kernel(x_ref, *refs):
    refs[-1][...] = x_ref[...]


def take(buffer, height, earlier):
    count, _, lanes = buffer.shape
    block = pl.BlockSpec((count // 2, height, lanes), lambda i: (i, 0, 0))
    return pl.pallas_call(
        take_kernel,
        out_shape=jax.ShapeDtypeStruct((count, height, lanes), buffer.dtype),
        grid=(2,),
        in_specs=[block] + [pl.BlockSpec(memory_space=pl.ANY)] * len(earlier),
        out_specs=block,
        name="take",
    )(buffer, *earlier)


def self_kernel(from_far, x_ref, *refs):
    o_ref = refs[-1]
    sources, local_len, head_size = o_ref.shape
    count = sources * local_len
    scale = head_size ** (-0.5) * log2e

    def slot(k):
        return x_ref[:, k * local_len : (k + 1) * local_len].reshape(count, head_size)

    ones = jnp.ones((count, head_size), jnp.bfloat16)
    keys = [slot(1), slot(4)]
    values = [jnp.concatenate([slot(k), ones], axis=1) for k in (2, 5)]
    queries = slot(3 * from_far)
    block = 2
    for at in range(0, sources, block):
        some = queries[at * local_len : (at + block) * local_len]
        scores = [nt_dot(some, k) for k in keys]
        top = jnp.maximum(*(jnp.max(s, axis=-1, keepdims=True) for s in scores))
        lifted = [jnp.exp2((s - top) * scale).astype(jnp.bfloat16) for s in scores]
        sums = [
            jnp.dot(l, v, preferred_element_type=jnp.float32) for l, v in zip(lifted, values)
        ]
        sums = sums[0] + sums[1]
        out = (sums[:, :head_size] / sums[:, head_size:]).astype(jnp.bfloat16)
        o_ref[at : at + block] = out.reshape(block, local_len, head_size)


def self_attention(packed, from_far, height, room, earlier):
    sources, _, head_size = packed.shape
    local_len = height // 3
    full_len = 2 * sources * local_len

    def kernel(*refs):
        self_kernel(from_far, *refs)

    return pl.pallas_call(
        kernel,
        out_shape=jax.ShapeDtypeStruct((sources, room, head_size), packed.dtype),
        grid=(1,),
        in_specs=[pl.BlockSpec((sources, 2 * height, head_size), lambda i: (0, 0, 0))]
        + [pl.BlockSpec(memory_space=pl.ANY)] * len(earlier),
        out_specs=pl.BlockSpec(
            (sources, local_len, head_size), lambda i: (0, room // local_len - 1, 0)
        ),
        compiler_params=params(),
        cost_estimate=pl.CostEstimate(
            flops=2 * full_len * full_len * head_size,
            bytes_accessed=6 * full_len * head_size,
            transcendentals=full_len * full_len // 2,
        ),
        name="self_attention",
    )(packed, *earlier)


def project_kernel(got_ref, other_ref, part_ref):
    sources, taken, feats = other_ref.shape
    head_size = part_ref.shape[-1] // 2
    per = 48
    blocks = taken // per
    for which, ref in enumerate((got_ref, other_ref)):
        squares = jnp.zeros((taken, 1), jnp.float32)
        total = [jnp.zeros((taken, head_size), jnp.float32) for _ in range(2)]
        for s in range(sources):
            block = ref[s, :taken].astype(jnp.float32)
            squares += jnp.sum(block * block, axis=-1, keepdims=True)
            after = taken + 2 * feats
            parts = got_ref[s, after : after + 16].astype(jnp.float32)
            gain = parts[0:1] + parts[1:2] + parts[2:3]
            scaled = (block * gain).astype(jnp.bfloat16)
            for k in range(2):
                at = taken + k * feats
                total[k] += jnp.dot(
                    scaled, got_ref[s, at : at + feats], preferred_element_type=jnp.float32
                )
        both = jnp.concatenate(total, axis=1)
        part_ref[which * taken : (which + 1) * taken] = both
        spread = jnp.broadcast_to(squares, (taken, 128)).T[:8]
        spread = jnp.concatenate([spread, jnp.zeros((8, 2 * head_size - taken))], axis=1)
        at = 2 * taken + 8 * which
        part_ref[at : at + 8] = spread


def project(got, other, head_size):
    sources, taken, feats = other.shape
    return pl.pallas_call(
        project_kernel,
        out_shape=jax.ShapeDtypeStruct((2 * taken + 16, 2 * head_size), jnp.float32),
        compiler_params=params(),
        cost_estimate=pl.CostEstimate(
            flops=8 * taken * sources * feats * head_size,
            bytes_accessed=4 * got.size,
            transcendentals=0,
        ),
        name="project",
    )(got, other)


def cross_kernel(full_width, q_ref, part_a, part_b, allowed_ref, far_ref, _, o_ref):
    sources, height, head_size = q_ref.shape
    videos = allowed_ref.shape[0]
    local_len = height // videos
    o_ref[:, height:] = far_ref[...]
    half = part_a.shape[0] // 2 - 8
    blocks, rows = 8, half // 4
    per = rows // videos
    inverse = []
    for which in range(2):
        at = 2 * half + 8 * which
        squares = part_a[at : at + 1, :half] + part_b[at : at + 1, :half]
        inv = lax.rsqrt(squares / full_width + norm_eps)
        inverse.append(jnp.broadcast_to(inv, (128, half)).T)
    kv = []
    for b in range(blocks):
        span = slice(b * rows, (b + 1) * rows)
        total = part_a[span] + part_b[span]
        at = (b % 4) * rows
        inv = inverse[b // 4][at : at + rows]
        kv.append(jnp.concatenate([total[:, :head_size] * inv, total[:, head_size:] * inv], axis=1))
    for v in range(videos):
        this = jnp.concatenate([blk[v * per : (v + 1) * per] for blk in kv], axis=0)
        this = this.astype(jnp.bfloat16)
        rows_of_v = slice(v * local_len, (v + 1) * local_len)
        for at in range(0, sources, 4):
            queries = q_ref[at : at + 4, rows_of_v].reshape(4 * local_len, head_size)
            scores = nt_dot(queries, this[:, :head_size])
            scores = jnp.where(allowed_ref[v, 0:1] > 0, scores, masked_score)
            out = softmax_dot(scores, this[:, head_size:], head_size ** (-0.5))
            o_ref[at : at + 4, rows_of_v] = out.reshape(4, local_len, head_size)


def cross_attention(packed, part, far_part, allowed, far_out, outs, height, full_width):
    sources, total, head_size = packed.shape
    taken = total - 2 * height
    count = sources * taken * allowed.shape[-1]

    def kernel(*refs):
        cross_kernel(full_width, *refs)

    return pl.pallas_call(
        kernel,
        out_shape=jax.ShapeDtypeStruct(outs.shape, outs.dtype),
        grid=(1,),
        in_specs=[pl.BlockSpec((sources, taken, head_size), lambda i: (0, 2 * height // taken, 0))]
        + [whole(one) for one in (part, far_part, allowed, far_out)]
        + [pl.BlockSpec(memory_space=pl.ANY)],
        out_specs=pl.BlockSpec(
            (sources, taken + far_out.shape[1], head_size), lambda i: (0, 0, 0)
        ),
        input_output_aliases={5: 0},
        compiler_params=params(),
        cost_estimate=pl.CostEstimate(
            flops=4 * count * head_size,
            bytes_accessed=4 * sources * taken * head_size,
            transcendentals=count,
        ),
        name="cross_attention",
    )(packed, part, far_part, allowed, far_out, outs)


def unpack_kernel(zh_ref, x_ref, self_ref, cross_ref):
    ny, pair, nx, local_len, head_size = self_ref.shape
    got = x_ref[...].reshape(ny, nx, 2 * pair * local_len, head_size)
    zh = zh_ref[0]
    for y in range(ny):
        for j in range(pair):
            cross_ref[y, j] = got[y, :, j * local_len : (j + 1) * local_len]
        self_ref[y, 1 - zh] = got[y, :, pair * local_len : (pair + 1) * local_len]
        self_ref[y, zh] = got[y, :, (pair + 1) * local_len :]


def unpack(zh, got, shape):
    ny, pair, nx, local_len, head_size = shape
    out = pl.BlockSpec((ny // 2,) + shape[1:], lambda i: (i, 0, 0, 0, 0))
    return pl.pallas_call(
        unpack_kernel,
        out_shape=(jax.ShapeDtypeStruct(shape, got.dtype),) * 2,
        grid=(2,),
        in_specs=[
            pl.BlockSpec(memory_space=pltpu.SMEM),
            pl.BlockSpec((ny // 2 * nx,) + got.shape[1:], lambda i: (i, 0, 0)),
        ],
        out_specs=(out, out),
        name="unpack",
    )(zh, got)


def hold_kernel(*refs):
    pass


def hold(value, earlier):
    return pl.pallas_call(
        hold_kernel,
        out_shape=jax.ShapeDtypeStruct(value.shape, value.dtype),
        in_specs=[pl.BlockSpec(memory_space=pl.ANY)] * (1 + len(earlier)),
        out_specs=pl.BlockSpec(memory_space=pl.ANY),
        input_output_aliases={0: 0},
        name="hold",
    )(value, *earlier)


def three_parts(values):
    high = lax.reduce_precision(values, 8, 7)
    rest = values - high
    middle = lax.reduce_precision(rest, 8, 7)
    return [p.astype(jnp.bfloat16) for p in (high, middle, rest - middle)]


def ahead(value, axis, step):
    return lax.ppermute(value, axis, [(i, (i + step) % 4) for i in range(4)])


def gather_ring(value, axis):
    return [value] + [ahead(value, axis, k) for k in (1, 3, 2)]


def ring_order(pieces):
    own, one, three, two = pieces
    return [own, one, two, three]


def body(video_qkv, cross_query, captions, caption_gain, key_value_weight, caption_lengths):
    videos, local_heads, local_len, slots, head_size = video_qkv.shape
    caption_len, feats = captions.shape[1:]
    ny, nx, nz = lax.axis_size("y"), lax.axis_size("x"), lax.axis_size("zl")
    pair, group, height = videos // ny, ny * nx, slots * local_len
    at_y, at_z, core = (lax.axis_index(a) for a in ("y", "zl", "c"))
    zh = lax.axis_index("zh").astype(jnp.int32).reshape(1)
    full_width = feats * group * 2

    items = video_qkv.transpose(0, 1, 3, 2, 4)
    items = items.reshape(ny, pair, nx, height, head_size)
    rows = ring_order(gather_ring(captions, "zl"))
    far = lax.ppermute(hold(pick(1 - zh, items), rows[1:]), "zh", SWAP)
    rows = jnp.stack(rows)
    rows = rows.reshape(nz, ny, pair * caption_len, feats).transpose(1, 0, 2, 3)
    taken = nz * pair * caption_len
    rows = rows.reshape(ny, 1, taken, feats)
    first = (at_z * 2 + core) * local_heads
    weights = lax.dynamic_slice_in_dim(key_value_weight, first, local_heads, axis=2)
    weights = weights.transpose(2, 1, 0, 3).reshape(1, nx, 2 * feats, head_size)
    gains = jnp.pad(jnp.stack(three_parts(caption_gain)), ((0, 13), (0, 0)))
    sent = jnp.concatenate(
        [
            jnp.broadcast_to(rows, (ny, nx, taken, feats)),
            jnp.broadcast_to(weights, (ny, nx, 2 * feats, head_size)),
            jnp.broadcast_to(gains, (ny, nx, 16, feats)),
        ],
        axis=2,
    ).reshape(group, taken + 2 * feats + 16, feats)
    got = lax.all_to_all(sent, XY, split_axis=0, concat_axis=0, tiled=True)
    queries = cross_query.reshape(ny, pair, nx, local_len, head_size)
    packed = hold(place(pack(zh, items, queries, []), far, 1), [got])
    other = lax.ppermute(take(got, taken, [packed]), "c", SWAP)
    part = project(got, other, head_size)
    far_part = lax.ppermute(part, "zh", SWAP)

    packed = lax.all_to_all(packed, XY, split_axis=0, concat_axis=0, tiled=True)

    far_out = self_attention(packed, 1, height, local_len, [part])
    far_out = lax.ppermute(far_out, "zh", SWAP)
    outs = self_attention(packed, 0, height, 2 * pair * local_len, [])

    which, z, token = jnp.meshgrid(
        jnp.arange(2), jnp.arange(nz), jnp.arange(caption_len), indexing="ij"
    )
    cores = jnp.where(which == 0, core, 1 - core)
    positions = (((at_z + nz - z) % nz * 2 + cores) * caption_len + token).reshape(-1)
    lengths = lax.dynamic_slice_in_dim(caption_lengths, at_y * pair, pair)
    allowed = (positions[None, :] < lengths[:, None]).astype(jnp.float32)
    allowed = jnp.broadcast_to(allowed[:, None, :], (pair, 8, allowed.shape[-1]))
    outs = cross_attention(packed, part, far_part, allowed, far_out, outs, height, full_width)
    outs = lax.all_to_all(outs, XY, split_axis=0, concat_axis=0, tiled=True)
    self_out, cross_out = unpack(zh, outs, (ny, pair, nx, local_len, head_size))
    shape = (videos, local_heads, local_len, head_size)
    return (self_out.reshape(shape), cross_out.reshape(shape))


def solution(mesh):
    devices = mesh.devices.reshape(4, 2, 4, 4, 2)
    placed = (
        P(None, TP, SEQ, None, None),
        P(None, TP, SEQ, None),
        P(None, TP, SEQ),
        P(SEQ),
        P(SEQ, None, None, None),
        P(),
    )
    return jax.shard_map(
        body,
        mesh=Mesh(devices, AXES),
        in_specs=placed,
        out_specs=(P(None, TP, SEQ, None), P(None, TP, SEQ, None)),
        check_vma=False,
    )
```

time: 195 us -> 134 us (0.69)
  the two profiles are of different devices: /device:TPU:66 before, /device:TPU:1 now
where the time goes in v2:
time: 134 us
  waiting for transfers between devices  41.4 us (31%)
  starting transfers between devices  33.2 us (25%)
  blocking collectives  29.3 us (22%)
  Pallas kernels  24.1 us (18%)
  local copies, waits for them, and re-layouts  3.2 us (2%)
  other arithmetic  1.55 us (1%)
    all_to_all x1, blocking collectives, body(): outs = lax.all_to_all(outs, XY, split_axis=0, concat_axis=0, tiled=True)  29.3 us
    ppermute x1, waiting for transfers between devices, body(): far = lax.ppermute(hold(pick(1 - zh, items), rows[1:]), 'zh', SWAP)  23 us
    all_to_all x1, waiting for transfers between devices, body(): packed = lax.all_to_all(packed, XY, split_axis=0, concat_axis=0, tiled=True)  13 us
    pallas_call x2, Pallas kernels, self_attention(): pl.pallas_call(kernel, out_shape=jax.ShapeDtypeStruct((sources, room, hea...  8.72 us
    all_to_all x1, starting transfers between devices, body(): packed = lax.all_to_all(packed, XY, split_axis=0, concat_axis=0, tiled=True)  6.81 us
    all_to_all x1, starting transfers between devices, body(): got = lax.all_to_all(sent, XY, split_axis=0, concat_axis=0, tiled=True)  6.8 us
    ppermute x3, starting transfers between devices, ahead(): return lax.ppermute(value, axis, [(i, (i + step) % 4) for i in range(4)])  5.63 us
    ppermute x1, starting transfers between devices, body(): far = lax.ppermute(hold(pick(1 - zh, items), rows[1:]), 'zh', SWAP)  4.21 us
  transfers between devices with their start and end apart: 9, of which 5 were waited for; matrix products, arithmetic and copies ran while one was open for 2% of the time, Pallas kernels for 15%

profile of v2, /device:TPU:1, one launch (start us, length us, event | category | flops | bytes accessed | tf_op | source)
XLA Modules:
  0.0 133.7 jit_solution(16452746316123376365)
XLA Ops:
  0.6 0.0 copy-start
  0.6 5.3 %collective-permute-start.2 = (bf16[8,24,128]{2,1,0:T(8,128)(2,1)}, bf16[8,24,128]{2,1,0:T(8,128)(2,1)S(1)}, u32[]{:S(2)}, u32[]{:S(2)}) collective-permute-start(bf16[8,24,128]{2,1,0:T(8,128)(2,1)} %param.8), channel_id=1, source_target_pairs={{0,6},{2,0},{4,2},{6,4},{1,7},{3,1},{5,3},{7,5},{8,14},{10,8},{12,... | collective-permute-start | bytes 147464 | tf_op jit(solution)/shard_map/ppermute | solution.py:349
  5.9 0.0 collective-permute-start
  5.9 0.4 collective-permute-start.1
  6.3 1.9 %pick.1.refs_0_ = bf16[16,192,128]{2,1,0:T(8,128)(2,1)} custom-call(s32[1]{0:T(128)S(6)} %sub.19.zh_ref, bf16[4,2,4,192,128]{4,3,2,1,0:T(8,128)(2,1)} %bitcast.31), custom_call_target="tpu_custom_call" | custom-call | tf_op jit(solution)/shard_map/pick/pallas_call | solution.py:47
  8.2 0.0 collective-permute-done.2.refs_3_
  8.2 2.6 %collective-permute-done.refs_1_ = bf16[8,24,128]{2,1,0:T(8,128)(2,1)S(1)} collective-permute-done((bf16[8,24,128]{2,1,0:T(8,128)(2,1)}, bf16[8,24,128]{2,1,0:T(8,128)(2,1)S(1)}, u32[]{:S(2)}, u32[]{:S(2)}) %collective-permute-start) | collective-permute-done | bytes 49184 | tf_op jit(solution)/shard_map/ppermute | solution.py:349
  10.8 0.0 collective-permute-done.1.refs_2_
  10.9 0.6 copy-done.3
  11.5 0.6 copy-done.5
  12.1 4.2 %collective-permute-start.3 = (bf16[16,192,128]{2,1,0:T(8,128)(2,1)}, bf16[16,192,128]{2,1,0:T(8,128)(2,1)S(1)}, u32[]{:S(2)}, u32[]{:S(2)}) collective-permute-start(bf16[16,192,128]{2,1,0:T(8,128)(2,1)} %hold.2), channel_id=1, source_target_pairs={{0,32},{32,0},{1,33},{33,1},{2,34},{34,2},{3,35},{35,3},{4,36},{36... | collective-permute-start | bytes 2359304 | tf_op jit(solution)/shard_map/ppermute | solution.py:373
  16.3 0.1 constant_dynamic-slice_fusion
  16.5 0.0 copy-start.8
  16.5 0.0 copy-start.4
  16.5 0.0 copy-start.6
  16.5 0.0 copy-start.7
  16.6 2.5 %pack.1._ = bf16[16,512,128]{2,1,0:T(8,128)(2,1)} custom-call(s32[1]{0:T(128)} %bitcast.zh_ref, bf16[4,2,4,192,128]{4,3,2,1,0:T(8,128)(2,1)} %bitcast.32, bf16[4,2,4,64,128]{4,3,2,1,0:T(8,128)(2,1)} %bitcast.35), custom_call_target="tpu_custom_call" | custom-call | tf_op jit(solution)/shard_map/pack/pallas_call | solution.py:79
  19.1 0.2 broadcast_in_dim.48
  19.4 0.1 broadcast_in_dim.46
  19.5 1.4 %pad_maximum_fusion = bf16[4,4,464,128]{3,2,1,0:T(8,128)(2,1)} fusion(bf16[4,4,16,128]{3,2,1,0:T(8,128)(2,1)S(1)} %broadcast_in_dim.49, bf16[4,4,256,128]{3,2,1,0:T(8,128)(2,1)S(1)} %broadcast_in_dim.48, bf16[4,4,192,128]{3,2,1,0:T(8,128)(2,1)S(1)} %broadcast_in_dim.46), kind=kLoop, calls=%fused_computation | loop fusion | flops 5701632 | bytes 3801088 | tf_op jit(solution)/shard_map/concatenate | solution.py:382
  20.9 6.8 %all-to-all-start = ((bf16[16,464,128]{2,1,0:T(8,128)(2,1)}), bf16[16,464,128]{2,1,0:T(8,128)(2,1)}, u32[]{:S(2)}, u32[]{:S(2)}) async-start(bf16[16,464,128]{2,1,0:T(8,128)(2,1)} %bitcast.30), calls=%async_computation | async-start | bytes 3801088 | tf_op jit(solution)/shard_map/all_to_all | solution.py:390
  27.7 23.0 %collective-permute-done.3.x_ref = bf16[16,192,128]{2,1,0:T(8,128)(2,1)S(1)} collective-permute-done((bf16[16,192,128]{2,1,0:T(8,128)(2,1)}, bf16[16,192,128]{2,1,0:T(8,128)(2,1)S(1)}, u32[]{:S(2)}, u32[]{:S(2)}) %collective-permute-start.3) | collective-permute-done | bytes 786464 | tf_op jit(solution)/shard_map/ppermute | solution.py:373
  50.8 0.9 copy-done.9
  51.7 1.9 %place.1.refs_0_ = bf16[16,512,128]{2,1,0:T(8,128)(2,1)} custom-call(bf16[16,192,128]{2,1,0:T(8,128)(2,1)} %copy-done.9, bf16[16,512,128]{2,1,0:T(8,128)(2,1)} %pack.1._), custom_call_target="tpu_custom_call", output_to_operand_aliasing={{}: (1, {})} | custom-call | flops 99999997952 | bytes 1572864 | tf_op jit(solution)/shard_map/place/pallas_call | solution.py:106
  53.6 0.0 all-to-all-done.refs_1_.x_ref.got_ref
  53.6 6.8 %all-to-all-start.1 = ((bf16[16,512,128]{2,1,0:T(8,128)(2,1)}), bf16[16,512,128]{2,1,0:T(8,128)(2,1)}, u32[]{:S(2)}, u32[]{:S(2)}) async-start(bf16[16,512,128]{2,1,0:T(8,128)(2,1)} %hold.3.refs_0_), calls=%async_computation.1 | async-start | bytes 4194304 | tf_op jit(solution)/shard_map/all_to_all | solution.py:397
  60.4 0.0 copy-start.10
  60.4 1.9 %take.1 = bf16[16,192,128]{2,1,0:T(8,128)(2,1)} custom-call(bf16[16,464,128]{2,1,0:T(8,128)(2,1)} %all-to-all-done.refs_1_.x_ref.got_ref, bf16[16,512,128]{2,1,0:T(8,128)(2,1)} %hold.3.refs_0_), custom_call_target="tpu_custom_call" | custom-call | tf_op jit(solution)/shard_map/take/pallas_call | solution.py:130
  62.4 2.8 %collective-permute-start.4 = (bf16[16,192,128]{2,1,0:T(8,128)(2,1)}, bf16[16,192,128]{2,1,0:T(8,128)(2,1)S(1)}, u32[]{:S(2)}, u32[]{:S(2)}) collective-permute-start(bf16[16,192,128]{2,1,0:T(8,128)(2,1)} %take.1), channel_id=1, source_target_pairs={{0,1},{1,0},{2,3},{3,2},{4,5},{5,4},{6,7},{7,6},{8,9},{9,8},{10,11... | collective-permute-start | bytes 2359304 | tf_op jit(solution)/shard_map/ppermute | solution.py:393
  65.2 0.1 broadcast_in_dim.54
  65.3 0.1 select_n.32
  65.4 0.1 broadcast_in_dim.50
  65.4 0.1 broadcast_in_dim.51
  65.5 0.1 broadcast_in_dim.56
  65.6 0.1 dynamic_slice.7
  65.7 1.6 %collective-permute-done.4.other_ref = bf16[16,192,128]{2,1,0:T(8,128)(2,1)S(1)} collective-permute-done((bf16[16,192,128]{2,1,0:T(8,128)(2,1)}, bf16[16,192,128]{2,1,0:T(8,128)(2,1)S(1)}, u32[]{:S(2)}, u32[]{:S(2)}) %collective-permute-start.4) | collective-permute-done | bytes 786464 | tf_op jit(solution)/shard_map/ppermute | solution.py:393
  67.3 2.5 %project.1.refs_1_ = f32[400,256]{1,0:T(8,128)S(1)} custom-call(bf16[16,464,128]{2,1,0:T(8,128)(2,1)} %all-to-all-done.refs_1_.x_ref.got_ref, bf16[16,192,128]{2,1,0:T(8,128)(2,1)S(1)} %collective-permute-done.4.other_ref), custom_call_target="tpu_custom_call" | custom-call | flops 402653184 | bytes 3801088 | tf_op jit(solution)/shard_map/project/pallas_call | solution.py:224
  69.8 3.0 %collective-permute-start.5 = (f32[400,256]{1,0:T(8,128)S(1)}, f32[400,256]{1,0:T(8,128)S(1)}, u32[]{:S(2)}, u32[]{:S(2)}) collective-permute-start(f32[400,256]{1,0:T(8,128)S(1)} %project.1.refs_1_), channel_id=1, source_target_pairs={{0,32},{32,0},{1,33},{33,1},{2,34},{34,2},{3,35},{35,3},{4,36},{36... | collective-permute-start | bytes 1228808 | tf_op jit(solution)/shard_map/ppermute | solution.py:395
  72.8 13.0 %all-to-all-done.1.refs_0_ = bf16[16,512,128]{2,1,0:T(8,128)(2,1)} async-done(((bf16[16,512,128]{2,1,0:T(8,128)(2,1)}), bf16[16,512,128]{2,1,0:T(8,128)(2,1)}, u32[]{:S(2)}, u32[]{:S(2)}) %all-to-all-start.1) | async-done | bytes 2097184 | tf_op jit(solution)/shard_map/all_to_all | solution.py:397
  85.9 4.3 %self_attention.2 = bf16[16,64,128]{2,1,0:T(8,128)(2,1)S(1)} custom-call(bf16[16,512,128]{2,1,0:T(8,128)(2,1)} %all-to-all-done.1.refs_0_, f32[400,256]{1,0:T(8,128)S(1)} %project.1.refs_1_), custom_call_target="tpu_custom_call" | custom-call | flops 1073741824 | bytes 1572864 | tf_op jit(solution)/shard_map/self_attention/pallas_call | solution.py:175
  90.2 4.0 %collective-permute-start.6 = (bf16[16,64,128]{2,1,0:T(8,128)(2,1)S(1)}, bf16[16,64,128]{2,1,0:T(8,128)(2,1)S(1)}, u32[]{:S(2)}, u32[]{:S(2)}) collective-permute-start(bf16[16,64,128]{2,1,0:T(8,128)(2,1)S(1)} %self_attention.2), channel_id=1, source_target_pairs={{0,32},{32,0},{1,33},{33,1},{2,34},{34,2},{3,35},{35,3},{4,36},{36... | collective-permute-start | bytes 786440 | tf_op jit(solution)/shard_map/ppermute | solution.py:400
  94.1 0.1 compare_convert_fusion
  94.2 4.4 %self_attention.3.refs_5_ = bf16[16,256,128]{2,1,0:T(8,128)(2,1)S(1)} custom-call(bf16[16,512,128]{2,1,0:T(8,128)(2,1)} %all-to-all-done.1.refs_0_), custom_call_target="tpu_custom_call" | custom-call | flops 1073741824 | bytes 1572864 | tf_op jit(solution)/shard_map/self_attention/pallas_call | solution.py:175
  98.6 0.0 collective-permute-done.5.refs_2_
  98.6 1.1 collective-permute-done.6.refs_4_
  99.8 2.5 %cross_attention.1 = bf16[16,256,128]{2,1,0:T(8,128)(2,1)S(1)} custom-call(bf16[16,512,128]{2,1,0:T(8,128)(2,1)} %all-to-all-done.1.refs_0_, f32[400,256]{1,0:T(8,128)S(1)} %project.1.refs_1_, f32[400,256]{1,0:T(8,128)S(1)} %collective-permute-done.5.refs_2_, f32[2,8,192]{2,1,0:T(8,128)S(1)} %broadcast_in_dim.57.refs_3_, ...), custom_call_target="tpu_custom_call", output_to_operand_aliasing={{}: (5, {})} | custom-call | flops 201326592 | bytes 1048576 | tf_op jit(solution)/shard_map/cross_attention/pallas_call | solution.py:278
  102.3 29.3 %all_to_all.15.x_ref = bf16[16,256,128]{2,1,0:T(8,128)(2,1)} all-to-all(bf16[16,256,128]{2,1,0:T(8,128)(2,1)S(1)} %cross_attention.1), channel_id=1, replica_groups=mesh['y'=4,'zh'=2,'x'=4,'zl'=4,'c'=2] {'y','x'}, dimensions={0} | all-to-all | bytes 2097152 | tf_op jit(solution)/shard_map/all_to_all | solution.py:412
  131.6 2.0 %unpack.1 = (bf16[4,2,4,64,128]{4,3,2,1,0:T(8,128)(2,1)}, bf16[4,2,4,64,128]{4,3,2,1,0:T(8,128)(2,1)}) custom-call(s32[1]{0:T(128)} %bitcast.zh_ref, bf16[16,256,128]{2,1,0:T(8,128)(2,1)} %all_to_all.15.x_ref), custom_call_target="tpu_custom_call" | custom-call | tf_op jit(solution)/shard_map/unpack/pallas_call | solution.py:313
  (25 shorter events, 0.1 us)
Async XLA Ops:
  0.6 15.7 %copy-start = (bf16[128,2,32,128]{3,2,1,0:T(8,128)(2,1)S(1)}, bf16[128,2,32,128]{3,2,1,0:T(8,128)(2,1)}, u32[]{:S(2)}) copy-start(bf16[128,2,32,128]{3,2,1,0:T(8,128)(2,1)} %param.10) | copy-start | bytes 6291460
  0.6 7.6 %collective-permute-start.2 = (bf16[8,24,128]{2,1,0:T(8,128)(2,1)}, bf16[8,24,128]{2,1,0:T(8,128)(2,1)S(1)}, u32[]{:S(2)}, u32[]{:S(2)}) collective-permute-start(bf16[8,24,128]{2,1,0:T(8,128)(2,1)} %param.8), channel_id=1, source_target_pairs={{0,6},{2,0},{4,2},{6,4},{1,7},{3,1},{5,3},{7,5},{8,14},{10,8},{12,... | collective-permute-start | bytes 147464 | tf_op jit(solution)/shard_map/ppermute | solution.py:349
  5.9 4.9 %collective-permute-start = (bf16[8,24,128]{2,1,0:T(8,128)(2,1)}, bf16[8,24,128]{2,1,0:T(8,128)(2,1)S(1)}, u32[]{:S(2)}, u32[]{:S(2)}) collective-permute-start(bf16[8,24,128]{2,1,0:T(8,128)(2,1)} %param.8), channel_id=1, source_target_pairs={{0,2},{2,4},{4,6},{6,0},{1,3},{3,5},{5,7},{7,1},{8,10},{10,12},{12... | collective-permute-start | bytes 147464 | tf_op jit(solution)/shard_map/ppermute | solution.py:349
  5.9 5.0 %collective-permute-start.1 = (bf16[8,24,128]{2,1,0:T(8,128)(2,1)}, bf16[8,24,128]{2,1,0:T(8,128)(2,1)S(1)}, u32[]{:S(2)}, u32[]{:S(2)}) collective-permute-start(bf16[8,24,128]{2,1,0:T(8,128)(2,1)} %param.8), channel_id=1, source_target_pairs={{0,4},{2,6},{4,0},{6,2},{1,5},{3,7},{5,1},{7,3},{8,12},{10,14},{12... | collective-permute-start | bytes 147464 | tf_op jit(solution)/shard_map/ppermute | solution.py:349
  8.2 2.6 %copy-start.1 = (bf16[8,24,128]{2,1,0:T(8,128)(2,1)}, bf16[8,24,128]{2,1,0:T(8,128)(2,1)S(1)}, u32[]{:S(2)}) copy-start(bf16[8,24,128]{2,1,0:T(8,128)(2,1)S(1)} %collective-permute-done.2.refs_3_) | copy-start | bytes 147460
  10.8 0.6 copy-start.3
  11.5 0.6 copy-start.5
  12.1 38.7 %collective-permute-start.3 = (bf16[16,192,128]{2,1,0:T(8,128)(2,1)}, bf16[16,192,128]{2,1,0:T(8,128)(2,1)S(1)}, u32[]{:S(2)}, u32[]{:S(2)}) collective-permute-start(bf16[16,192,128]{2,1,0:T(8,128)(2,1)} %hold.2), channel_id=1, source_target_pairs={{0,32},{32,0},{1,33},{33,1},{2,34},{34,2},{3,35},{35,3},{4,36},{36... | collective-permute-start | bytes 2359304 | tf_op jit(solution)/shard_map/ppermute | solution.py:373
  16.5 2.6 %copy-start.8 = (f32[128]{0:T(128)S(1)}, f32[128]{0:T(128)}, u32[]{:S(2)}) copy-start(f32[128]{0:T(128)} %param.9) | copy-start | bytes 1540
  16.5 2.6 %copy-start.2 = (bf16[8,24,128]{2,1,0:T(8,128)(2,1)S(1)}, bf16[8,24,128]{2,1,0:T(8,128)(2,1)}, u32[]{:S(2)}) copy-start(bf16[8,24,128]{2,1,0:T(8,128)(2,1)} %copy-done.1) | copy-start | bytes 147460
  16.5 2.6 %copy-start.4 = (bf16[8,24,128]{2,1,0:T(8,128)(2,1)S(1)}, bf16[8,24,128]{2,1,0:T(8,128)(2,1)}, u32[]{:S(2)}) copy-start(bf16[8,24,128]{2,1,0:T(8,128)(2,1)} %copy-done.3) | copy-start | bytes 147460
  16.5 2.6 %copy-start.6 = (bf16[8,24,128]{2,1,0:T(8,128)(2,1)S(1)}, bf16[8,24,128]{2,1,0:T(8,128)(2,1)}, u32[]{:S(2)}) copy-start(bf16[8,24,128]{2,1,0:T(8,128)(2,1)} %copy-done.5) | copy-start | bytes 147460
  16.5 2.6 %copy-start.7 = (bf16[8,24,128]{2,1,0:T(8,128)(2,1)S(1)}, bf16[8,24,128]{2,1,0:T(8,128)(2,1)}, u32[]{:S(2)}) copy-start(bf16[8,24,128]{2,1,0:T(8,128)(2,1)} %param.8) | copy-start | bytes 147460
  20.9 32.7 %all-to-all-start = ((bf16[16,464,128]{2,1,0:T(8,128)(2,1)}), bf16[16,464,128]{2,1,0:T(8,128)(2,1)}, u32[]{:S(2)}, u32[]{:S(2)}) async-start(bf16[16,464,128]{2,1,0:T(8,128)(2,1)} %bitcast.30), calls=%async_computation | async-start | bytes 3801088 | tf_op jit(solution)/shard_map/all_to_all | solution.py:390
  50.8 0.9 copy-start.9
  53.6 32.3 %all-to-all-start.1 = ((bf16[16,512,128]{2,1,0:T(8,128)(2,1)}), bf16[16,512,128]{2,1,0:T(8,128)(2,1)}, u32[]{:S(2)}, u32[]{:S(2)}) async-start(bf16[16,512,128]{2,1,0:T(8,128)(2,1)} %hold.3.refs_0_), calls=%async_computation.1 | async-start | bytes 4194304 | tf_op jit(solution)/shard_map/all_to_all | solution.py:397
  60.4 5.2 %copy-start.10 = (s32[8]{0:T(128)S(1)}, s32[8]{0:T(128)}, u32[]{:S(2)}) copy-start(s32[8]{0:T(128)} %param.11) | copy-start | bytes 100
  62.4 4.9 %collective-permute-start.4 = (bf16[16,192,128]{2,1,0:T(8,128)(2,1)}, bf16[16,192,128]{2,1,0:T(8,128)(2,1)S(1)}, u32[]{:S(2)}, u32[]{:S(2)}) collective-permute-start(bf16[16,192,128]{2,1,0:T(8,128)(2,1)} %take.1), channel_id=1, source_target_pairs={{0,1},{1,0},{2,3},{3,2},{4,5},{5,4},{6,7},{7,6},{8,9},{9,8},{10,11... | collective-permute-start | bytes 2359304 | tf_op jit(solution)/shard_map/ppermute | solution.py:393
  69.8 28.8 %collective-permute-start.5 = (f32[400,256]{1,0:T(8,128)S(1)}, f32[400,256]{1,0:T(8,128)S(1)}, u32[]{:S(2)}, u32[]{:S(2)}) collective-permute-start(f32[400,256]{1,0:T(8,128)S(1)} %project.1.refs_1_), channel_id=1, source_target_pairs={{0,32},{32,0},{1,33},{33,1},{2,34},{34,2},{3,35},{35,3},{4,36},{36... | collective-permute-start | bytes 1228808 | tf_op jit(solution)/shard_map/ppermute | solution.py:395
  90.2 9.6 %collective-permute-start.6 = (bf16[16,64,128]{2,1,0:T(8,128)(2,1)S(1)}, bf16[16,64,128]{2,1,0:T(8,128)(2,1)S(1)}, u32[]{:S(2)}, u32[]{:S(2)}) collective-permute-start(bf16[16,64,128]{2,1,0:T(8,128)(2,1)S(1)} %self_attention.2), channel_id=1, source_target_pairs={{0,32},{32,0},{1,33},{33,1},{2,34},{34,2},{3,35},{35,3},{4,36},{36... | collective-permute-start | bytes 786440 | tf_op jit(solution)/shard_map/ppermute | solution.py:400

commit v3 on v2

--- a/solution.py
+++ b/solution.py
@@ -14,7 +14,7 @@
 XY = ("y", "x")
 TP = ("zl", "c")
 SWAP = [(0, 1), (1, 0)]
-PLACE_FLOPS = 100_000_000_000
+BUILD_FLOPS = 100_000_000_000
 VMEM_LIMIT = 40 * 1024 * 1024
 
 
@@ -38,15 +38,17 @@
     return pl.BlockSpec(array.shape, lambda *_: (0,) * array.ndim)
 
 
-def pick_kernel(zh_ref, x_ref, o_ref):
-    o_ref[...] = x_ref[...].reshape(o_ref.shape)
-
-
-def pick(zh, items):
+def pick_kernel(zh_ref, x_ref, *refs):
+    o_ref = refs[-1]
+    ny, _, nx, height, lanes = x_ref.shape
+    o_ref[:, :height] = x_ref[...].reshape(ny * nx, height, lanes)
+
+
+def pick(zh, items, runs, earlier):
     ny, _, nx, height, lanes = items.shape
     return pl.pallas_call(
         pick_kernel,
-        out_shape=jax.ShapeDtypeStruct((ny * nx, height, lanes), items.dtype),
+        out_shape=jax.ShapeDtypeStruct((ny * nx, runs * height, lanes), items.dtype),
         grid_spec=pltpu.PrefetchScalarGridSpec(
             num_scalar_prefetch=1,
             grid=(2,),
@@ -54,31 +56,25 @@
                 pl.BlockSpec(
                     (ny // 2, 1, nx, height, lanes), lambda i, zh_ref: (i, zh_ref[0], 0, 0, 0)
                 )
-            ],
+            ]
+            + [pl.BlockSpec(memory_space=pl.ANY)] * len(earlier),
             out_specs=pl.BlockSpec((ny // 2 * nx, height, lanes), lambda i, zh_ref: (i, 0, 0)),
         ),
         name="pick",
-    )(zh, items)
-
-
-def pack_kernel(zh_ref, x_ref, q_ref, *refs):
-    o_ref = refs[-1]
+    )(zh, items, *earlier)
+
+
+def build_kernel(zh_ref, x_ref, far_ref, o_ref):
     ny, _, nx, height, lanes = x_ref.shape
-    pair, local_len = q_ref.shape[1], q_ref.shape[3]
     o_ref[:, :height] = x_ref[...].reshape(ny * nx, height, lanes)
-    for y in range(ny):
-        for j in range(pair):
-            at = 2 * height + j * local_len
-            o_ref[y * nx : (y + 1) * nx, at : at + local_len] = q_ref[y, j]
-
-
-def pack(zh, items, queries, earlier):
+    o_ref[:, height:] = far_ref[...]
+
+
+def build(zh, items, far):
     ny, _, nx, height, lanes = items.shape
-    pair, local_len = queries.shape[1], queries.shape[3]
-    total = 2 * height + pair * local_len
-    return pl.pallas_call(
-        pack_kernel,
-        out_shape=jax.ShapeDtypeStruct((ny * nx, total, lanes), items.dtype),
+    return pl.pallas_call(
+        build_kernel,
+        out_shape=jax.ShapeDtypeStruct((ny * nx, 2 * height, lanes), items.dtype),
         grid_spec=pltpu.PrefetchScalarGridSpec(
             num_scalar_prefetch=1,
             grid=(2,),
@@ -86,15 +82,15 @@
                 pl.BlockSpec(
                     (ny // 2, 1, nx, height, lanes), lambda i, zh_ref: (i, zh_ref[0], 0, 0, 0)
                 ),
-                pl.BlockSpec(
-                    (ny // 2, pair, nx, local_len, lanes), lambda i, zh_ref: (i, 0, 0, 0, 0)
-                ),
-            ]
-            + [pl.BlockSpec(memory_space=pl.ANY)] * len(earlier),
-            out_specs=pl.BlockSpec((ny // 2 * nx, total, lanes), lambda i, zh_ref: (i, 0, 0)),
-        ),
-        name="pack",
-    )(zh, items, queries, *earlier)
+                pl.BlockSpec((ny // 2 * nx, height, lanes), lambda i, zh_ref: (i, 0, 0)),
+            ],
+            out_specs=pl.BlockSpec((ny // 2 * nx, 2 * height, lanes), lambda i, zh_ref: (i, 0, 0)),
+        ),
+        cost_estimate=pl.CostEstimate(
+            flops=BUILD_FLOPS, bytes_accessed=4 * items.size, transcendentals=0
+        ),
+        name="build",
+    )(zh, items, far)
 
 
 def place_kernel(x_ref, _, o_ref):
@@ -113,26 +109,24 @@
         ],
         out_specs=pl.BlockSpec((count // 2, height, lanes), lambda i: (i, at, 0)),
         input_output_aliases={1: 0},
-        cost_estimate=pl.CostEstimate(
-            flops=PLACE_FLOPS, bytes_accessed=4 * part.size, transcendentals=0
-        ),
         name="place",
     )(part, buffer)
 
 
 def take_kernel(x_ref, *refs):
-    refs[-1][...] = x_ref[...]
-
-
-def take(buffer, height, earlier):
+    o_ref = refs[-1]
+    o_ref[...] = x_ref[:, x_ref.shape[1] - o_ref.shape[1] :]
+
+
+def take(buffer, first, height, earlier):
     count, _, lanes = buffer.shape
-    block = pl.BlockSpec((count // 2, height, lanes), lambda i: (i, 0, 0))
     return pl.pallas_call(
         take_kernel,
         out_shape=jax.ShapeDtypeStruct((count, height, lanes), buffer.dtype),
         grid=(2,),
-        in_specs=[block] + [pl.BlockSpec(memory_space=pl.ANY)] * len(earlier),
-        out_specs=block,
+        in_specs=[pl.BlockSpec((count // 2, first + height, lanes), lambda i: (i, 0, 0))]
+        + [pl.BlockSpec(memory_space=pl.ANY)] * len(earlier),
+        out_specs=pl.BlockSpec((count // 2, height, lanes), lambda i: (i, 0, 0)),
         name="take",
     )(buffer, *earlier)
 
@@ -164,23 +158,26 @@
         o_ref[at : at + block] = out.reshape(block, local_len, head_size)
 
 
-def self_attention(packed, from_far, height, room, earlier):
-    sources, _, head_size = packed.shape
-    local_len = height // 3
+def self_attention(packed, from_far, earlier, into=None):
+    sources, total, head_size = packed.shape
+    local_len = total // 6
     full_len = 2 * sources * local_len
 
     def kernel(*refs):
         self_kernel(from_far, *refs)
 
+    room = local_len if into is None else into.shape[1]
+    given = list(earlier) if into is None else [into] + list(earlier)
     return pl.pallas_call(
         kernel,
         out_shape=jax.ShapeDtypeStruct((sources, room, head_size), packed.dtype),
         grid=(1,),
-        in_specs=[pl.BlockSpec((sources, 2 * height, head_size), lambda i: (0, 0, 0))]
-        + [pl.BlockSpec(memory_space=pl.ANY)] * len(earlier),
+        in_specs=[whole(packed)]
+        + [pl.BlockSpec(memory_space=pl.ANY)] * len(given),
         out_specs=pl.BlockSpec(
             (sources, local_len, head_size), lambda i: (0, room // local_len - 1, 0)
         ),
+        input_output_aliases={} if into is None else {1: 0},
         compiler_params=params(),
         cost_estimate=pl.CostEstimate(
             flops=2 * full_len * full_len * head_size,
@@ -188,42 +185,53 @@
             transcendentals=full_len * full_len // 2,
         ),
         name="self_attention",
-    )(packed, *earlier)
-
-
-def project_kernel(got_ref, other_ref, part_ref):
-    sources, taken, feats = other_ref.shape
+    )(packed, *given)
+
+
+def project_kernel(w_first, got_ref, mine_ref, other_ref, part_ref, sent_ref):
+    sources, taken, feats = mine_ref.shape
     head_size = part_ref.shape[-1] // 2
-    per = 48
-    blocks = taken // per
-    for which, ref in enumerate((got_ref, other_ref)):
+    for which, ref in enumerate((mine_ref, other_ref)):
         squares = jnp.zeros((taken, 1), jnp.float32)
         total = [jnp.zeros((taken, head_size), jnp.float32) for _ in range(2)]
         for s in range(sources):
-            block = ref[s, :taken].astype(jnp.float32)
+            block = ref[s].astype(jnp.float32)
             squares += jnp.sum(block * block, axis=-1, keepdims=True)
-            after = taken + 2 * feats
+            after = w_first + 2 * feats
             parts = got_ref[s, after : after + 16].astype(jnp.float32)
             gain = parts[0:1] + parts[1:2] + parts[2:3]
             scaled = (block * gain).astype(jnp.bfloat16)
             for k in range(2):
-                at = taken + k * feats
+                at = w_first + k * feats
                 total[k] += jnp.dot(
                     scaled, got_ref[s, at : at + feats], preferred_element_type=jnp.float32
                 )
         both = jnp.concatenate(total, axis=1)
         part_ref[which * taken : (which + 1) * taken] = both
-        spread = jnp.broadcast_to(squares, (taken, 128)).T[:8]
-        spread = jnp.concatenate([spread, jnp.zeros((8, 2 * head_size - taken))], axis=1)
-        at = 2 * taken + 8 * which
-        part_ref[at : at + 8] = spread
-
-
-def project(got, other, head_size):
-    sources, taken, feats = other.shape
-    return pl.pallas_call(
-        project_kernel,
-        out_shape=jax.ShapeDtypeStruct((2 * taken + 16, 2 * head_size), jnp.float32),
+        sent_ref[which * taken : (which + 1) * taken] = both.astype(jnp.bfloat16)
+        spread = jnp.broadcast_to(squares, (taken, 128)).T[:16]
+        spread = jnp.concatenate([spread, jnp.zeros((16, 2 * head_size - taken))], axis=1)
+        at = 2 * taken + 16 * which
+        part_ref[at : at + 16] = spread
+        for k in range(3):
+            high = spread.astype(jnp.bfloat16)
+            spread = spread - high.astype(jnp.float32)
+            at = 2 * taken + 16 * (2 * k + which)
+            sent_ref[at : at + 16] = high
+
+
+def project(got, w_first, mine, other, head_size):
+    sources, taken, feats = mine.shape
+
+    def kernel(*refs):
+        project_kernel(w_first, *refs)
+
+    return pl.pallas_call(
+        kernel,
+        out_shape=(
+            jax.ShapeDtypeStruct((2 * taken + 32, 2 * head_size), jnp.float32),
+            jax.ShapeDtypeStruct((2 * taken + 96, 2 * head_size), jnp.bfloat16),
+        ),
         compiler_params=params(),
         cost_estimate=pl.CostEstimate(
             flops=8 * taken * sources * feats * head_size,
@@ -231,27 +239,29 @@
             transcendentals=0,
         ),
         name="project",
-    )(got, other)
-
-
-def cross_kernel(full_width, q_ref, part_a, part_b, allowed_ref, far_ref, _, o_ref):
-    sources, height, head_size = q_ref.shape
-    videos = allowed_ref.shape[0]
-    local_len = height // videos
-    o_ref[:, height:] = far_ref[...]
-    half = part_a.shape[0] // 2 - 8
+    )(got, mine, other)
+
+
+def cross_kernel(full_width, *refs):
+    q_refs, (part_a, part_b, allowed_ref, o_ref) = refs[:-4], refs[-4:]
+    sources, local_len, head_size = q_refs[0].shape
+    videos = len(q_refs)
+    half = part_a.shape[0] // 2 - 16
     blocks, rows = 8, half // 4
     per = rows // videos
     inverse = []
     for which in range(2):
-        at = 2 * half + 8 * which
-        squares = part_a[at : at + 1, :half] + part_b[at : at + 1, :half]
+        at = 2 * half + 16 * which
+        squares = part_a[at : at + 16, :half]
+        for k in range(3):
+            squares += part_b[at + 32 * k : at + 32 * k + 16, :half].astype(jnp.float32)
+        squares = squares[:1]
         inv = lax.rsqrt(squares / full_width + norm_eps)
         inverse.append(jnp.broadcast_to(inv, (128, half)).T)
     kv = []
     for b in range(blocks):
         span = slice(b * rows, (b + 1) * rows)
-        total = part_a[span] + part_b[span]
+        total = part_a[span] + part_b[span].astype(jnp.float32)
         at = (b % 4) * rows
         inv = inverse[b // 4][at : at + rows]
         kv.append(jnp.concatenate([total[:, :head_size] * inv, total[:, head_size:] * inv], axis=1))
@@ -260,16 +270,16 @@
         this = this.astype(jnp.bfloat16)
         rows_of_v = slice(v * local_len, (v + 1) * local_len)
         for at in range(0, sources, 4):
-            queries = q_ref[at : at + 4, rows_of_v].reshape(4 * local_len, head_size)
+            queries = q_refs[v][at : at + 4].reshape(4 * local_len, head_size)
             scores = nt_dot(queries, this[:, :head_size])
             scores = jnp.where(allowed_ref[v, 0:1] > 0, scores, masked_score)
             out = softmax_dot(scores, this[:, head_size:], head_size ** (-0.5))
             o_ref[at : at + 4, rows_of_v] = out.reshape(4, local_len, head_size)
 
 
-def cross_attention(packed, part, far_part, allowed, far_out, outs, height, full_width):
-    sources, total, head_size = packed.shape
-    taken = total - 2 * height
+def cross_attention(got, part, far_part, allowed, pair, local_len, room, full_width):
+    sources, _, head_size = got.shape
+    taken = pair * local_len
     count = sources * taken * allowed.shape[-1]
 
     def kernel(*refs):
@@ -277,15 +287,14 @@
 
     return pl.pallas_call(
         kernel,
-        out_shape=jax.ShapeDtypeStruct(outs.shape, outs.dtype),
+        out_shape=jax.ShapeDtypeStruct((sources, room, head_size), got.dtype),
         grid=(1,),
-        in_specs=[pl.BlockSpec((sources, taken, head_size), lambda i: (0, 2 * height // taken, 0))]
-        + [whole(one) for one in (part, far_part, allowed, far_out)]
-        + [pl.BlockSpec(memory_space=pl.ANY)],
-        out_specs=pl.BlockSpec(
-            (sources, taken + far_out.shape[1], head_size), lambda i: (0, 0, 0)
-        ),
-        input_output_aliases={5: 0},
+        in_specs=[
+            pl.BlockSpec((sources, local_len, head_size), lambda i, at=at: (0, at, 0))
+            for at in range(pair)
+        ]
+        + [whole(one) for one in (part, far_part, allowed)],
+        out_specs=pl.BlockSpec((sources, taken, head_size), lambda i: (0, 0, 0)),
         compiler_params=params(),
         cost_estimate=pl.CostEstimate(
             flops=4 * count * head_size,
@@ -293,7 +302,7 @@
             transcendentals=count,
         ),
         name="cross_attention",
-    )(packed, part, far_part, allowed, far_out, outs)
+    )(*[got] * pair, part, far_part, allowed)
 
 
 def unpack_kernel(zh_ref, x_ref, self_ref, cross_ref):
@@ -370,35 +379,36 @@
     items = video_qkv.transpose(0, 1, 3, 2, 4)
     items = items.reshape(ny, pair, nx, height, head_size)
     rows = ring_order(gather_ring(captions, "zl"))
-    far = lax.ppermute(hold(pick(1 - zh, items), rows[1:]), "zh", SWAP)
-    rows = jnp.stack(rows)
-    rows = rows.reshape(nz, ny, pair * caption_len, feats).transpose(1, 0, 2, 3)
-    taken = nz * pair * caption_len
+    far = pick(1 - zh, items, 1, [])
+    far = lax.ppermute(hold(far, rows[1:]), "zh", SWAP)
+    rows = jnp.stack(rows).reshape(nz, ny, pair * caption_len, feats).transpose(1, 0, 2, 3)
+    taken, asked = nz * pair * caption_len, pair * local_len
     rows = rows.reshape(ny, 1, taken, feats)
+    queries = cross_query.reshape(ny, pair, nx, local_len, head_size).transpose(0, 2, 1, 3, 4)
     first = (at_z * 2 + core) * local_heads
     weights = lax.dynamic_slice_in_dim(key_value_weight, first, local_heads, axis=2)
     weights = weights.transpose(2, 1, 0, 3).reshape(1, nx, 2 * feats, head_size)
     gains = jnp.pad(jnp.stack(three_parts(caption_gain)), ((0, 13), (0, 0)))
     sent = jnp.concatenate(
         [
+            queries.reshape(ny, nx, asked, head_size),
             jnp.broadcast_to(rows, (ny, nx, taken, feats)),
             jnp.broadcast_to(weights, (ny, nx, 2 * feats, head_size)),
             jnp.broadcast_to(gains, (ny, nx, 16, feats)),
         ],
         axis=2,
-    ).reshape(group, taken + 2 * feats + 16, feats)
+    ).reshape(group, asked + taken + 2 * feats + 16, feats)
     got = lax.all_to_all(sent, XY, split_axis=0, concat_axis=0, tiled=True)
-    queries = cross_query.reshape(ny, pair, nx, local_len, head_size)
-    packed = hold(place(pack(zh, items, queries, []), far, 1), [got])
-    other = lax.ppermute(take(got, taken, [packed]), "c", SWAP)
-    part = project(got, other, head_size)
-    far_part = lax.ppermute(part, "zh", SWAP)
-
+
+    packed = hold(build(zh, items, far), [got])
+    mine = take(got, asked, taken, [packed])
+    other = lax.ppermute(mine, "c", SWAP)
+    part, part_sent = project(got, asked + taken, mine, other, head_size)
+    far_part = lax.ppermute(part_sent, "zh", SWAP)
     packed = lax.all_to_all(packed, XY, split_axis=0, concat_axis=0, tiled=True)
 
-    far_out = self_attention(packed, 1, height, local_len, [part])
+    far_out = self_attention(packed, 1, [part])
     far_out = lax.ppermute(far_out, "zh", SWAP)
-    outs = self_attention(packed, 0, height, 2 * pair * local_len, [])
 
     which, z, token = jnp.meshgrid(
         jnp.arange(2), jnp.arange(nz), jnp.arange(caption_len), indexing="ij"
@@ -408,7 +418,9 @@
     lengths = lax.dynamic_slice_in_dim(caption_lengths, at_y * pair, pair)
     allowed = (positions[None, :] < lengths[:, None]).astype(jnp.float32)
     allowed = jnp.broadcast_to(allowed[:, None, :], (pair, 8, allowed.shape[-1]))
-    outs = cross_attention(packed, part, far_part, allowed, far_out, outs, height, full_width)
+    outs = cross_attention(got, part, far_part, allowed, pair, local_len, 2 * asked, full_width)
+    outs = self_attention(packed, 0, [], outs)
+    outs = place(outs, far_out, pair)
     outs = lax.all_to_all(outs, XY, split_axis=0, concat_axis=0, tiled=True)
     self_out, cross_out = unpack(zh, outs, (ny, pair, nx, local_len, head_size))
     shape = (videos, local_heads, local_len, head_size)

time: 134 us -> 131 us (0.978)
  the two profiles are of different devices: /device:TPU:1 before, /device:TPU:64 now
where the time goes in v3:
time: 131 us
  waiting for transfers between devices  50.6 us (39%)
  starting transfers between devices  24.8 us (19%)
  Pallas kernels  24 us (18%)
  blocking collectives  22.5 us (17%)
  local copies, waits for them, and re-layouts  5.03 us (4%)
  other arithmetic  3.11 us (2%)
    ppermute x1, waiting for transfers between devices, body(): far = lax.ppermute(hold(far, rows[1:]), 'zh', SWAP)  25.4 us
    all_to_all x1, blocking collectives, body(): outs = lax.all_to_all(outs, XY, split_axis=0, concat_axis=0, tiled=True)  22.5 us
    all_to_all x1, waiting for transfers between devices, body(): packed = lax.all_to_all(packed, XY, split_axis=0, concat_axis=0, tiled=True)  11.6 us
    pallas_call x2, Pallas kernels, self_attention(): pl.pallas_call(kernel, out_shape=jax.ShapeDtypeStruct((sources, room, hea...  8.72 us
    all_to_all x1, starting transfers between devices, body(): got = lax.all_to_all(sent, XY, split_axis=0, concat_axis=0, tiled=True)  7.08 us
    all_to_all x1, waiting for transfers between devices, body(): got = lax.all_to_all(sent, XY, split_axis=0, concat_axis=0, tiled=True)  6.06 us
    ppermute x1, starting transfers between devices, body(): far = lax.ppermute(hold(far, rows[1:]), 'zh', SWAP)  4.95 us
    all_to_all x1, starting transfers between devices, body(): packed = lax.all_to_all(packed, XY, split_axis=0, concat_axis=0, tiled=True)  4.4 us
  transfers between devices with their start and end apart: 9, of which 7 were waited for; matrix products, arithmetic and copies ran while one was open for 4% of the time, Pallas kernels for 16%

profile of v3, /device:TPU:64, one launch (start us, length us, event | category | flops | bytes accessed | tf_op | source)
XLA Modules:
  0.0 130.9 jit_solution(1791744089971898860)
XLA Ops:
  0.6 0.0 copy-start
  0.6 1.5 %collective-permute-start.1 = (bf16[8,24,128]{2,1,0:T(8,128)(2,1)}, bf16[8,24,128]{2,1,0:T(8,128)(2,1)S(1)}, u32[]{:S(2)}, u32[]{:S(2)}) collective-permute-start(bf16[8,24,128]{2,1,0:T(8,128)(2,1)} %param.8), channel_id=1, source_target_pairs={{0,4},{2,6},{4,0},{6,2},{1,5},{3,7},{5,1},{7,3},{8,12},{10,14},{12... | collective-permute-start | bytes 147464 | tf_op jit(solution)/shard_map/ppermute | solution.py:358
  2.1 2.0 %collective-permute-start.2 = (bf16[8,24,128]{2,1,0:T(8,128)(2,1)}, bf16[8,24,128]{2,1,0:T(8,128)(2,1)S(1)}, u32[]{:S(2)}, u32[]{:S(2)}) collective-permute-start(bf16[8,24,128]{2,1,0:T(8,128)(2,1)} %param.8), channel_id=1, source_target_pairs={{0,6},{2,0},{4,2},{6,4},{1,7},{3,1},{5,3},{7,5},{8,14},{10,8},{12,... | collective-permute-start | bytes 147464 | tf_op jit(solution)/shard_map/ppermute | solution.py:358
  4.1 0.0 collective-permute-start
  4.2 2.0 %pick.1.refs_0_ = bf16[16,192,128]{2,1,0:T(8,128)(2,1)} custom-call(s32[1]{0:T(128)S(6)} %sub.19.zh_ref, bf16[4,2,4,192,128]{4,3,2,1,0:T(8,128)(2,1)} %bitcast.37), custom_call_target="tpu_custom_call" | custom-call | tf_op jit(solution)/shard_map/pick/pallas_call | solution.py:49
  6.2 0.0 collective-permute-done.1.refs_2_
  6.2 0.2 collective-permute-done.2.refs_3_
  6.4 2.1 %collective-permute-done.refs_1_ = bf16[8,24,128]{2,1,0:T(8,128)(2,1)S(1)} collective-permute-done((bf16[8,24,128]{2,1,0:T(8,128)(2,1)}, bf16[8,24,128]{2,1,0:T(8,128)(2,1)S(1)}, u32[]{:S(2)}, u32[]{:S(2)}) %collective-permute-start) | collective-permute-done | bytes 49184 | tf_op jit(solution)/shard_map/ppermute | solution.py:358
  8.6 0.6 copy-done.7
  9.2 4.9 %collective-permute-start.3 = (bf16[16,192,128]{2,1,0:T(8,128)(2,1)}, bf16[16,192,128]{2,1,0:T(8,128)(2,1)}, u32[]{:S(2)}, u32[]{:S(2)}) collective-permute-start(bf16[16,192,128]{2,1,0:T(8,128)(2,1)} %hold.2), channel_id=1, source_target_pairs={{0,32},{32,0},{1,33},{33,1},{2,34},{34,2},{3,35},{35,3},{4,36},{36... | collective-permute-start | bytes 2359304 | tf_op jit(solution)/shard_map/ppermute | solution.py:383
  14.1 0.1 constant_dynamic-slice_fusion
  14.4 0.9 pad_maximum_fusion.1
  15.3 0.2 broadcast_in_dim.48
  15.5 0.1 broadcast_in_dim.46
  15.7 1.6 %pad_maximum_fusion = bf16[16,592,128]{2,1,0:T(8,128)(2,1)} fusion(bf16[16,16,128]{2,1,0:T(8,128)(2,1)S(1)} %broadcast_in_dim.49, bf16[16,256,128]{2,1,0:T(8,128)(2,1)S(1)} %bitcast.34, bf16[16,192,128]{2,1,0:T(8,128)(2,1)S(1)} %bitcast.35, bf16[16,128,128]{2,1,0:T(8,128)(2,1)S(1)} %bitcast.36), kind=kLoop, calls=%fused_computation | loop fusion | flops 9699328 | bytes 4849664 | tf_op jit(solution)/shard_map/concatenate | solution.py:392
  17.3 7.1 %all-to-all-start = ((bf16[16,592,128]{2,1,0:T(8,128)(2,1)}), bf16[16,592,128]{2,1,0:T(8,128)(2,1)}, u32[]{:S(2)}, u32[]{:S(2)}) async-start(bf16[16,592,128]{2,1,0:T(8,128)(2,1)} %pad_maximum_fusion), calls=%async_computation | async-start | bytes 4849664 | tf_op jit(solution)/shard_map/all_to_all | solution.py:401
  24.3 25.4 %collective-permute-done.3.far_ref = bf16[16,192,128]{2,1,0:T(8,128)(2,1)} collective-permute-done((bf16[16,192,128]{2,1,0:T(8,128)(2,1)}, bf16[16,192,128]{2,1,0:T(8,128)(2,1)}, u32[]{:S(2)}, u32[]{:S(2)}) %collective-permute-start.3) | collective-permute-done | bytes 786464 | tf_op jit(solution)/shard_map/ppermute | solution.py:383
  49.7 2.4 %build.1.refs_0_ = bf16[16,384,128]{2,1,0:T(8,128)(2,1)} custom-call(s32[1]{0:T(128)} %bitcast.zh_ref, bf16[4,2,4,192,128]{4,3,2,1,0:T(8,128)(2,1)} %bitcast.38, bf16[16,192,128]{2,1,0:T(8,128)(2,1)} %collective-permute-done.3.far_ref), custom_call_target="tpu_custom_call" | custom-call | flops 99999997952 | bytes 3145728 | tf_op jit(solution)/shard_map/build/pallas_call | solution.py:75
  52.1 6.1 %all-to-all-done.refs_1_.x_ref.refs_0_ = bf16[16,592,128]{2,1,0:T(8,128)(2,1)} async-done(((bf16[16,592,128]{2,1,0:T(8,128)(2,1)}), bf16[16,592,128]{2,1,0:T(8,128)(2,1)}, u32[]{:S(2)}, u32[]{:S(2)}) %all-to-all-start) | async-done | bytes 2424864 | tf_op jit(solution)/shard_map/all_to_all | solution.py:401
  58.1 4.4 %all-to-all-start.1 = ((bf16[16,384,128]{2,1,0:T(8,128)(2,1)}), bf16[16,384,128]{2,1,0:T(8,128)(2,1)}, u32[]{:S(2)}, u32[]{:S(2)}) async-start(bf16[16,384,128]{2,1,0:T(8,128)(2,1)} %hold.3.refs_0_), calls=%async_computation.1 | async-start | bytes 3145728 | tf_op jit(solution)/shard_map/all_to_all | solution.py:408
  62.5 0.0 copy-start.12
  62.6 2.1 %take.1.refs_1_ = bf16[16,192,128]{2,1,0:T(8,128)(2,1)} custom-call(bf16[16,592,128]{2,1,0:T(8,128)(2,1)} %all-to-all-done.refs_1_.x_ref.refs_0_, bf16[16,384,128]{2,1,0:T(8,128)(2,1)} %hold.3.refs_0_), custom_call_target="tpu_custom_call" | custom-call | tf_op jit(solution)/shard_map/take/pallas_call | solution.py:123
  64.7 0.0 collective-permute-start.4
  64.7 0.1 broadcast_in_dim.54
  64.8 0.1 select_n.32
  64.9 0.1 broadcast_in_dim.50
  64.9 0.1 broadcast_in_dim.51
  65.0 0.1 broadcast_in_dim.56
  65.1 0.6 dynamic_slice.7
  65.7 0.6 multiply_add_fusion
  66.3 0.9 collective-permute-done.4.refs_2_
  67.2 1.1 copy-done.2
  68.3 2.7 %project.1 = (f32[416,256]{1,0:T(8,128)S(1)}, bf16[480,256]{1,0:T(8,128)(2,1)S(1)}) custom-call(bf16[16,592,128]{2,1,0:T(8,128)(2,1)} %all-to-all-done.refs_1_.x_ref.refs_0_, bf16[16,192,128]{2,1,0:T(8,128)(2,1)S(1)} %copy-done.2, bf16[16,192,128]{2,1,0:T(8,128)(2,1)S(1)} %collective-permute-done.4.refs_2_), custom_call_target="tpu_custom_call" | custom-call | flops 402653184 | bytes 4849664 | tf_op jit(solution)/shard_map/project/pallas_call | solution.py:229
  71.0 0.0 copy-start.9
  71.0 0.0 copy-start.10
  71.0 2.5 %collective-permute-start.6 = (bf16[480,256]{1,0:T(8,128)(2,1)S(1)}, bf16[480,256]{1,0:T(8,128)(2,1)S(1)}, u32[]{:S(2)}, u32[]{:S(2)}) collective-permute-start(bf16[480,256]{1,0:T(8,128)(2,1)S(1)} %get-tuple-element.7), channel_id=1, source_target_pairs={{0,32},{32,0},{1,33},{33,1},{2,34},{34,2},{3,35},{35,3},{4,36},{36... | collective-permute-start | bytes 737288 | tf_op jit(solution)/shard_map/ppermute | solution.py:407
  73.5 11.6 %all-to-all-done.1.refs_0_ = bf16[16,384,128]{2,1,0:T(8,128)(2,1)} async-done(((bf16[16,384,128]{2,1,0:T(8,128)(2,1)}), bf16[16,384,128]{2,1,0:T(8,128)(2,1)}, u32[]{:S(2)}, u32[]{:S(2)}) %all-to-all-start.1) | async-done | bytes 1572896 | tf_op jit(solution)/shard_map/all_to_all | solution.py:408
  85.1 4.3 %self_attention.2 = bf16[16,64,128]{2,1,0:T(8,128)(2,1)S(1)} custom-call(bf16[16,384,128]{2,1,0:T(8,128)(2,1)} %all-to-all-done.1.refs_0_, f32[416,256]{1,0:T(8,128)S(1)} %get-tuple-element.6.refs_1_.refs_2_), custom_call_target="tpu_custom_call" | custom-call | flops 1073741824 | bytes 1572864 | tf_op jit(solution)/shard_map/self_attention/pallas_call | solution.py:171
  89.4 2.4 %collective-permute-start.5 = (bf16[16,64,128]{2,1,0:T(8,128)(2,1)S(1)}, bf16[16,64,128]{2,1,0:T(8,128)(2,1)S(1)}, u32[]{:S(2)}, u32[]{:S(2)}) collective-permute-start(bf16[16,64,128]{2,1,0:T(8,128)(2,1)S(1)} %self_attention.2), channel_id=1, source_target_pairs={{0,32},{32,0},{1,33},{33,1},{2,34},{34,2},{3,35},{35,3},{4,36},{36... | collective-permute-start | bytes 786440 | tf_op jit(solution)/shard_map/ppermute | solution.py:411
  91.8 0.1 compare_convert_fusion
  91.9 2.5 %cross_attention.1.refs_1_ = bf16[16,256,128]{2,1,0:T(8,128)(2,1)S(1)} custom-call(bf16[16,592,128]{2,1,0:T(8,128)(2,1)} %all-to-all-done.refs_1_.x_ref.refs_0_, bf16[16,592,128]{2,1,0:T(8,128)(2,1)} %all-to-all-done.refs_1_.x_ref.refs_0_, f32[416,256]{1,0:T(8,128)S(1)} %get-tuple-element.6.refs_1_.refs_2_, ...), custom_call_target="tpu_custom_call" | custom-call | flops 201326592 | bytes 1048576 | tf_op jit(solution)/shard_map/cross_attention/pallas_call | solution.py:288
  94.3 4.4 %self_attention.3._ = bf16[16,256,128]{2,1,0:T(8,128)(2,1)S(1)} custom-call(bf16[16,384,128]{2,1,0:T(8,128)(2,1)} %all-to-all-done.1.refs_0_, bf16[16,256,128]{2,1,0:T(8,128)(2,1)S(1)} %cross_attention.1.refs_1_), custom_call_target="tpu_custom_call", output_to_operand_aliasing={{}: (1, {})} | custom-call | flops 1073741824 | bytes 1572864 | tf_op jit(solution)/shard_map/self_attention/pallas_call | solution.py:171
  98.7 1.0 copy-done.1
  99.7 4.3 %collective-permute-done.5.x_ref = bf16[16,64,128]{2,1,0:T(8,128)(2,1)S(1)} collective-permute-done((bf16[16,64,128]{2,1,0:T(8,128)(2,1)S(1)}, bf16[16,64,128]{2,1,0:T(8,128)(2,1)S(1)}, u32[]{:S(2)}, u32[]{:S(2)}) %collective-permute-start.5) | collective-permute-done | bytes 262176 | tf_op jit(solution)/shard_map/ppermute | solution.py:411
  104.0 0.7 copy-done.4
  104.7 1.6 %place.1 = bf16[16,256,128]{2,1,0:T(8,128)(2,1)} custom-call(bf16[16,64,128]{2,1,0:T(8,128)(2,1)} %copy-done.4, bf16[16,256,128]{2,1,0:T(8,128)(2,1)} %copy-done.1), custom_call_target="tpu_custom_call", output_to_operand_aliasing={{}: (1, {})} | custom-call | tf_op jit(solution)/shard_map/place/pallas_call | solution.py:102
  106.3 22.5 %all_to_all.15.x_ref = bf16[16,256,128]{2,1,0:T(8,128)(2,1)} all-to-all(bf16[16,256,128]{2,1,0:T(8,128)(2,1)} %place.1), channel_id=1, replica_groups=mesh['y'=4,'zh'=2,'x'=4,'zl'=4,'c'=2] {'y','x'}, dimensions={0} | all-to-all | bytes 2097152 | tf_op jit(solution)/shard_map/all_to_all | solution.py:424
  128.8 2.0 %unpack.1 = (bf16[4,2,4,64,128]{4,3,2,1,0:T(8,128)(2,1)}, bf16[4,2,4,64,128]{4,3,2,1,0:T(8,128)(2,1)}) custom-call(s32[1]{0:T(128)} %bitcast.zh_ref, bf16[16,256,128]{2,1,0:T(8,128)(2,1)} %all_to_all.15.x_ref), custom_call_target="tpu_custom_call" | custom-call | tf_op jit(solution)/shard_map/unpack/pallas_call | solution.py:322
  (30 shorter events, 0.2 us)
Async XLA Ops:
  0.6 13.5 %copy-start = (bf16[128,2,32,128]{3,2,1,0:T(8,128)(2,1)S(1)}, bf16[128,2,32,128]{3,2,1,0:T(8,128)(2,1)}, u32[]{:S(2)}) copy-start(bf16[128,2,32,128]{3,2,1,0:T(8,128)(2,1)} %param.10) | copy-start | bytes 6291460
  0.6 5.5 %collective-permute-start.1 = (bf16[8,24,128]{2,1,0:T(8,128)(2,1)}, bf16[8,24,128]{2,1,0:T(8,128)(2,1)S(1)}, u32[]{:S(2)}, u32[]{:S(2)}) collective-permute-start(bf16[8,24,128]{2,1,0:T(8,128)(2,1)} %param.8), channel_id=1, source_target_pairs={{0,4},{2,6},{4,0},{6,2},{1,5},{3,7},{5,1},{7,3},{8,12},{10,14},{12... | collective-permute-start | bytes 147464 | tf_op jit(solution)/shard_map/ppermute | solution.py:358
  2.1 4.3 %collective-permute-start.2 = (bf16[8,24,128]{2,1,0:T(8,128)(2,1)}, bf16[8,24,128]{2,1,0:T(8,128)(2,1)S(1)}, u32[]{:S(2)}, u32[]{:S(2)}) collective-permute-start(bf16[8,24,128]{2,1,0:T(8,128)(2,1)} %param.8), channel_id=1, source_target_pairs={{0,6},{2,0},{4,2},{6,4},{1,7},{3,1},{5,3},{7,5},{8,14},{10,8},{12,... | collective-permute-start | bytes 147464 | tf_op jit(solution)/shard_map/ppermute | solution.py:358
  4.1 4.5 %collective-permute-start = (bf16[8,24,128]{2,1,0:T(8,128)(2,1)}, bf16[8,24,128]{2,1,0:T(8,128)(2,1)S(1)}, u32[]{:S(2)}, u32[]{:S(2)}) collective-permute-start(bf16[8,24,128]{2,1,0:T(8,128)(2,1)} %param.8), channel_id=1, source_target_pairs={{0,2},{2,4},{4,6},{6,0},{1,3},{3,5},{5,7},{7,1},{8,10},{10,12},{12... | collective-permute-start | bytes 147464 | tf_op jit(solution)/shard_map/ppermute | solution.py:358
  4.1 10.2 %copy-start.3 = (bf16[8,4,64,128]{3,2,1,0:T(8,128)(2,1)S(1)}, bf16[8,4,64,128]{3,2,1,0:T(8,128)(2,1)}, u32[]{:S(2)}) copy-start(bf16[8,4,64,128]{3,2,1,0:T(8,128)(2,1)} %param.7) | copy-start | bytes 1572868
  6.1 8.2 %copy-start.11 = (f32[128]{0:T(128)S(1)}, f32[128]{0:T(128)}, u32[]{:S(2)}) copy-start(f32[128]{0:T(128)} %param.9) | copy-start | bytes 1540
  6.2 8.3 %copy-start.8 = (bf16[8,24,128]{2,1,0:T(8,128)(2,1)S(1)}, bf16[8,24,128]{2,1,0:T(8,128)(2,1)}, u32[]{:S(2)}) copy-start(bf16[8,24,128]{2,1,0:T(8,128)(2,1)} %param.8) | copy-start | bytes 147460
  6.2 2.4 %copy-start.5 = (bf16[8,24,128]{2,1,0:T(8,128)(2,1)}, bf16[8,24,128]{2,1,0:T(8,128)(2,1)S(1)}, u32[]{:S(2)}) copy-start(bf16[8,24,128]{2,1,0:T(8,128)(2,1)S(1)} %collective-permute-done.1.refs_2_) | copy-start | bytes 147460
  6.4 2.1 %copy-start.6 = (bf16[8,24,128]{2,1,0:T(8,128)(2,1)}, bf16[8,24,128]{2,1,0:T(8,128)(2,1)S(1)}, u32[]{:S(2)}) copy-start(bf16[8,24,128]{2,1,0:T(8,128)(2,1)S(1)} %collective-permute-done.2.refs_3_) | copy-start | bytes 147460
  8.6 0.6 copy-start.7
  9.2 40.5 %collective-permute-start.3 = (bf16[16,192,128]{2,1,0:T(8,128)(2,1)}, bf16[16,192,128]{2,1,0:T(8,128)(2,1)}, u32[]{:S(2)}, u32[]{:S(2)}) collective-permute-start(bf16[16,192,128]{2,1,0:T(8,128)(2,1)} %hold.2), channel_id=1, source_target_pairs={{0,32},{32,0},{1,33},{33,1},{2,34},{34,2},{3,35},{35,3},{4,36},{36... | collective-permute-start | bytes 2359304 | tf_op jit(solution)/shard_map/ppermute | solution.py:383
  17.3 40.9 %all-to-all-start = ((bf16[16,592,128]{2,1,0:T(8,128)(2,1)}), bf16[16,592,128]{2,1,0:T(8,128)(2,1)}, u32[]{:S(2)}, u32[]{:S(2)}) async-start(bf16[16,592,128]{2,1,0:T(8,128)(2,1)} %pad_maximum_fusion), calls=%async_computation | async-start | bytes 4849664 | tf_op jit(solution)/shard_map/all_to_all | solution.py:401
  58.1 26.9 %all-to-all-start.1 = ((bf16[16,384,128]{2,1,0:T(8,128)(2,1)}), bf16[16,384,128]{2,1,0:T(8,128)(2,1)}, u32[]{:S(2)}, u32[]{:S(2)}) async-start(bf16[16,384,128]{2,1,0:T(8,128)(2,1)} %hold.3.refs_0_), calls=%async_computation.1 | async-start | bytes 3145728 | tf_op jit(solution)/shard_map/all_to_all | solution.py:408
  62.5 2.6 %copy-start.12 = (s32[8]{0:T(128)S(1)}, s32[8]{0:T(128)}, u32[]{:S(2)}) copy-start(s32[8]{0:T(128)} %param.11) | copy-start | bytes 100
  64.7 2.5 %collective-permute-start.4 = (bf16[16,192,128]{2,1,0:T(8,128)(2,1)}, bf16[16,192,128]{2,1,0:T(8,128)(2,1)S(1)}, u32[]{:S(2)}, u32[]{:S(2)}) collective-permute-start(bf16[16,192,128]{2,1,0:T(8,128)(2,1)} %take.1.refs_1_), channel_id=1, source_target_pairs={{0,1},{1,0},{2,3},{3,2},{4,5},{5,4},{6,7},{7,6},{8,9},{9,8},{10,11... | collective-permute-start | bytes 2359304 | tf_op jit(solution)/shard_map/ppermute | solution.py:405
  67.2 1.1 copy-start.2
  71.0 20.8 %copy-start.9 = (s32[192]{0:T(256)S(1)}, s32[192]{0:T(256)}, u32[]{:S(2)}) copy-start(s32[192]{0:T(256)} %multiply_add_fusion) | copy-start | bytes 2308
  71.0 20.8 %copy-start.10 = (s32[2]{0:T(128)S(1)}, s32[2]{0:T(128)}, u32[]{:S(2)}) copy-start(s32[2]{0:T(128)} %dynamic_slice.7) | copy-start | bytes 28
  71.0 20.9 %collective-permute-start.6 = (bf16[480,256]{1,0:T(8,128)(2,1)S(1)}, bf16[480,256]{1,0:T(8,128)(2,1)S(1)}, u32[]{:S(2)}, u32[]{:S(2)}) collective-permute-start(bf16[480,256]{1,0:T(8,128)(2,1)S(1)} %get-tuple-element.7), channel_id=1, source_target_pairs={{0,32},{32,0},{1,33},{33,1},{2,34},{34,2},{3,35},{35,3},{4,36},{36... | collective-permute-start | bytes 737288 | tf_op jit(solution)/shard_map/ppermute | solution.py:407
  89.4 14.6 %collective-permute-start.5 = (bf16[16,64,128]{2,1,0:T(8,128)(2,1)S(1)}, bf16[16,64,128]{2,1,0:T(8,128)(2,1)S(1)}, u32[]{:S(2)}, u32[]{:S(2)}) collective-permute-start(bf16[16,64,128]{2,1,0:T(8,128)(2,1)S(1)} %self_attention.2), channel_id=1, source_target_pairs={{0,32},{32,0},{1,33},{33,1},{2,34},{34,2},{3,35},{35,3},{4,36},{36... | collective-permute-start | bytes 786440 | tf_op jit(solution)/shard_map/ppermute | solution.py:411
  98.7 1.0 copy-start.1
  104.0 0.7 copy-start.4

commit v4 on v3

--- a/solution.py
+++ b/solution.py
@@ -91,26 +91,6 @@
         ),
         name="build",
     )(zh, items, far)
-
-
-def place_kernel(x_ref, _, o_ref):
-    o_ref[...] = x_ref[...]
-
-
-def place(buffer, part, at):
-    count, height, lanes = part.shape
-    return pl.pallas_call(
-        place_kernel,
-        out_shape=jax.ShapeDtypeStruct(buffer.shape, buffer.dtype),
-        grid=(2,),
-        in_specs=[
-            pl.BlockSpec((count // 2, height, lanes), lambda i: (i, 0, 0)),
-            pl.BlockSpec(memory_space=pl.ANY),
-        ],
-        out_specs=pl.BlockSpec((count // 2, height, lanes), lambda i: (i, at, 0)),
-        input_output_aliases={1: 0},
-        name="place",
-    )(part, buffer)
 
 
 def take_kernel(x_ref, *refs):
@@ -418,9 +398,9 @@
     lengths = lax.dynamic_slice_in_dim(caption_lengths, at_y * pair, pair)
     allowed = (positions[None, :] < lengths[:, None]).astype(jnp.float32)
     allowed = jnp.broadcast_to(allowed[:, None, :], (pair, 8, allowed.shape[-1]))
-    outs = cross_attention(got, part, far_part, allowed, pair, local_len, 2 * asked, full_width)
-    outs = self_attention(packed, 0, [], outs)
-    outs = place(outs, far_out, pair)
+    crossed = cross_attention(got, part, far_part, allowed, pair, local_len, asked, full_width)
+    near_out = self_attention(packed, 0, [crossed])
+    outs = jnp.concatenate([crossed, far_out, near_out], axis=1)
     outs = lax.all_to_all(outs, XY, split_axis=0, concat_axis=0, tiled=True)
     self_out, cross_out = unpack(zh, outs, (ny, pair, nx, local_len, head_size))
     shape = (videos, local_heads, local_len, head_size)

time: 131 us -> 130 us (level)
  the two profiles are of different devices: /device:TPU:64 before, /device:TPU:1 now
where the time goes in v4:
time: 130 us
  waiting for transfers between devices  46.3 us (36%)
  starting transfers between devices  29.5 us (23%)
  blocking collectives  23.7 us (18%)
  Pallas kernels  22.1 us (17%)
  local copies, waits for them, and re-layouts  3.97 us (3%)
  other arithmetic  3.19 us (2%)
    ppermute x1, waiting for transfers between devices, body(): far = lax.ppermute(hold(far, rows[1:]), 'zh', SWAP)  24.6 us
    all_to_all x1, blocking collectives, body(): outs = lax.all_to_all(outs, XY, split_axis=0, concat_axis=0, tiled=True)  23.7 us
    all_to_all x1, waiting for transfers between devices, body(): packed = lax.all_to_all(packed, XY, split_axis=0, concat_axis=0, tiled=True)  9.58 us
    pallas_call x2, Pallas kernels, self_attention(): pl.pallas_call(kernel, out_shape=jax.ShapeDtypeStruct((sources, room, hea...  8.61 us
    all_to_all x1, starting transfers between devices, body(): packed = lax.all_to_all(packed, XY, split_axis=0, concat_axis=0, tiled=True)  8.3 us
    all_to_all x1, starting transfers between devices, body(): got = lax.all_to_all(sent, XY, split_axis=0, concat_axis=0, tiled=True)  6.8 us
    ppermute x1, waiting for transfers between devices, body(): far_out = lax.ppermute(far_out, 'zh', SWAP)  6.33 us
    ppermute x3, starting transfers between devices, ahead(): return lax.ppermute(value, axis, [(i, (i + step) % 4) for i in range(4)])  5.63 us
  transfers between devices with their start and end apart: 9, of which 6 were waited for; matrix products, arithmetic and copies ran while one was open for 4% of the time, Pallas kernels for 15%

profile of v4, /device:TPU:1, one launch (start us, length us, event | category | flops | bytes accessed | tf_op | source)
XLA Modules:
  0.0 129.5 jit_solution(7182250358780815069)
XLA Ops:
  0.6 0.0 copy-start
  0.6 5.3 %collective-permute-start.2 = (bf16[8,24,128]{2,1,0:T(8,128)(2,1)}, bf16[8,24,128]{2,1,0:T(8,128)(2,1)S(1)}, u32[]{:S(2)}, u32[]{:S(2)}) collective-permute-start(bf16[8,24,128]{2,1,0:T(8,128)(2,1)} %param.8), channel_id=1, source_target_pairs={{0,6},{2,0},{4,2},{6,4},{1,7},{3,1},{5,3},{7,5},{8,14},{10,8},{12,... | collective-permute-start | bytes 147464 | tf_op jit(solution)/shard_map/ppermute | solution.py:338
  5.9 0.0 collective-permute-start
  5.9 0.4 collective-permute-start.1
  6.3 2.0 %pick.1.refs_0_ = bf16[16,192,128]{2,1,0:T(8,128)(2,1)} custom-call(s32[1]{0:T(128)S(6)} %sub.21.zh_ref, bf16[4,2,4,192,128]{4,3,2,1,0:T(8,128)(2,1)} %bitcast.37), custom_call_target="tpu_custom_call" | custom-call | tf_op jit(solution)/shard_map/pick/pallas_call | solution.py:49
  8.3 0.0 collective-permute-done.2.refs_3_
  8.3 2.6 %collective-permute-done.refs_1_ = bf16[8,24,128]{2,1,0:T(8,128)(2,1)S(1)} collective-permute-done((bf16[8,24,128]{2,1,0:T(8,128)(2,1)}, bf16[8,24,128]{2,1,0:T(8,128)(2,1)S(1)}, u32[]{:S(2)}, u32[]{:S(2)}) %collective-permute-start) | collective-permute-done | bytes 49184 | tf_op jit(solution)/shard_map/ppermute | solution.py:338
  10.8 0.0 collective-permute-done.1.refs_2_
  10.9 0.6 copy-done.4
  11.5 0.6 copy-done.5
  12.1 4.2 %collective-permute-start.3 = (bf16[16,192,128]{2,1,0:T(8,128)(2,1)}, bf16[16,192,128]{2,1,0:T(8,128)(2,1)}, u32[]{:S(2)}, u32[]{:S(2)}) collective-permute-start(bf16[16,192,128]{2,1,0:T(8,128)(2,1)} %hold.2), channel_id=1, source_target_pairs={{0,32},{32,0},{1,33},{33,1},{2,34},{34,2},{3,35},{35,3},{4,36},{36... | collective-permute-start | bytes 2359304 | tf_op jit(solution)/shard_map/ppermute | solution.py:363
  16.3 0.1 constant_dynamic-slice_fusion
  16.6 0.9 pad_maximum_fusion.2
  17.5 0.2 broadcast_in_dim.48
  17.7 0.1 broadcast_in_dim.46
  17.9 1.6 %pad_maximum_fusion = bf16[16,592,128]{2,1,0:T(8,128)(2,1)} fusion(bf16[16,16,128]{2,1,0:T(8,128)(2,1)S(1)} %broadcast_in_dim.49, bf16[16,256,128]{2,1,0:T(8,128)(2,1)S(1)} %bitcast.34, bf16[16,192,128]{2,1,0:T(8,128)(2,1)S(1)} %bitcast.35, bf16[16,128,128]{2,1,0:T(8,128)(2,1)S(1)} %bitcast.36), kind=kLoop, calls=%fused_computation | loop fusion | flops 9699328 | bytes 4849664 | tf_op jit(solution)/shard_map/concatenate | solution.py:372
  19.4 6.8 %all-to-all-start = ((bf16[16,592,128]{2,1,0:T(8,128)(2,1)}), bf16[16,592,128]{2,1,0:T(8,128)(2,1)}, u32[]{:S(2)}, u32[]{:S(2)}) async-start(bf16[16,592,128]{2,1,0:T(8,128)(2,1)} %pad_maximum_fusion), calls=%async_computation | async-start | bytes 4849664 | tf_op jit(solution)/shard_map/all_to_all | solution.py:381
  26.2 24.6 %collective-permute-done.3.far_ref = bf16[16,192,128]{2,1,0:T(8,128)(2,1)} collective-permute-done((bf16[16,192,128]{2,1,0:T(8,128)(2,1)}, bf16[16,192,128]{2,1,0:T(8,128)(2,1)}, u32[]{:S(2)}, u32[]{:S(2)}) %collective-permute-start.3) | collective-permute-done | bytes 786464 | tf_op jit(solution)/shard_map/ppermute | solution.py:363
  50.9 2.4 %build.1.refs_0_ = bf16[16,384,128]{2,1,0:T(8,128)(2,1)} custom-call(s32[1]{0:T(128)} %bitcast.zh_ref, bf16[4,2,4,192,128]{4,3,2,1,0:T(8,128)(2,1)} %bitcast.38, bf16[16,192,128]{2,1,0:T(8,128)(2,1)} %collective-permute-done.3.far_ref), custom_call_target="tpu_custom_call" | custom-call | flops 99999997952 | bytes 3145728 | tf_op jit(solution)/shard_map/build/pallas_call | solution.py:75
  53.2 2.6 %all-to-all-done.refs_1_.x_ref.refs_0_ = bf16[16,592,128]{2,1,0:T(8,128)(2,1)} async-done(((bf16[16,592,128]{2,1,0:T(8,128)(2,1)}), bf16[16,592,128]{2,1,0:T(8,128)(2,1)}, u32[]{:S(2)}, u32[]{:S(2)}) %all-to-all-start) | async-done | bytes 2424864 | tf_op jit(solution)/shard_map/all_to_all | solution.py:381
  55.9 8.3 %all-to-all-start.1 = ((bf16[16,384,128]{2,1,0:T(8,128)(2,1)}), bf16[16,384,128]{2,1,0:T(8,128)(2,1)}, u32[]{:S(2)}, u32[]{:S(2)}) async-start(bf16[16,384,128]{2,1,0:T(8,128)(2,1)} %hold.3.refs_0_), calls=%async_computation.1 | async-start | bytes 3145728 | tf_op jit(solution)/shard_map/all_to_all | solution.py:388
  64.2 0.0 copy-start.10
  64.2 2.1 %take.1.refs_1_ = bf16[16,192,128]{2,1,0:T(8,128)(2,1)} custom-call(bf16[16,592,128]{2,1,0:T(8,128)(2,1)} %all-to-all-done.refs_1_.x_ref.refs_0_, bf16[16,384,128]{2,1,0:T(8,128)(2,1)} %hold.3.refs_0_), custom_call_target="tpu_custom_call" | custom-call | tf_op jit(solution)/shard_map/take/pallas_call | solution.py:103
  66.3 1.9 %collective-permute-start.4 = (bf16[16,192,128]{2,1,0:T(8,128)(2,1)}, bf16[16,192,128]{2,1,0:T(8,128)(2,1)S(1)}, u32[]{:S(2)}, u32[]{:S(2)}) collective-permute-start(bf16[16,192,128]{2,1,0:T(8,128)(2,1)} %take.1.refs_1_), channel_id=1, source_target_pairs={{0,1},{1,0},{2,3},{3,2},{4,5},{5,4},{6,7},{7,6},{8,9},{9,8},{10,11... | collective-permute-start | bytes 2359304 | tf_op jit(solution)/shard_map/ppermute | solution.py:385
  68.2 0.1 broadcast_in_dim.54
  68.3 0.1 select_n.32
  68.4 0.1 broadcast_in_dim.50
  68.4 0.1 broadcast_in_dim.51
  68.5 0.1 broadcast_in_dim.56
  68.6 0.6 dynamic_slice.7
  69.2 0.6 multiply_add_fusion
  69.8 0.5 collective-permute-done.4.refs_2_
  70.3 1.1 copy-done.1
  71.5 2.7 %project.1 = (f32[416,256]{1,0:T(8,128)S(1)}, bf16[480,256]{1,0:T(8,128)(2,1)S(1)}) custom-call(bf16[16,592,128]{2,1,0:T(8,128)(2,1)} %all-to-all-done.refs_1_.x_ref.refs_0_, bf16[16,192,128]{2,1,0:T(8,128)(2,1)S(1)} %copy-done.1, bf16[16,192,128]{2,1,0:T(8,128)(2,1)S(1)} %collective-permute-done.4.refs_2_), custom_call_target="tpu_custom_call" | custom-call | flops 402653184 | bytes 4849664 | tf_op jit(solution)/shard_map/project/pallas_call | solution.py:209
  74.1 0.0 copy-start.7
  74.1 0.0 copy-start.8
  74.1 1.2 collective-permute-start.5
  75.4 9.6 %all-to-all-done.1.refs_0_ = bf16[16,384,128]{2,1,0:T(8,128)(2,1)} async-done(((bf16[16,384,128]{2,1,0:T(8,128)(2,1)}), bf16[16,384,128]{2,1,0:T(8,128)(2,1)}, u32[]{:S(2)}, u32[]{:S(2)}) %all-to-all-start.1) | async-done | bytes 1572896 | tf_op jit(solution)/shard_map/all_to_all | solution.py:388
  85.0 4.3 %self_attention.2 = bf16[16,64,128]{2,1,0:T(8,128)(2,1)S(1)} custom-call(bf16[16,384,128]{2,1,0:T(8,128)(2,1)} %all-to-all-done.1.refs_0_, f32[416,256]{1,0:T(8,128)S(1)} %get-tuple-element.6.refs_2_.refs_1_), custom_call_target="tpu_custom_call" | custom-call | flops 1073741824 | bytes 1572864 | tf_op jit(solution)/shard_map/self_attention/pallas_call | solution.py:151
  89.3 1.4 %collective-permute-start.6 = (bf16[16,64,128]{2,1,0:T(8,128)(2,1)S(1)}, bf16[16,64,128]{2,1,0:T(8,128)(2,1)S(1)}, u32[]{:S(2)}, u32[]{:S(2)}) collective-permute-start(bf16[16,64,128]{2,1,0:T(8,128)(2,1)S(1)} %self_attention.2), channel_id=1, source_target_pairs={{0,32},{32,0},{1,33},{33,1},{2,34},{34,2},{3,35},{35,3},{4,36},{36... | collective-permute-start | bytes 786440 | tf_op jit(solution)/shard_map/ppermute | solution.py:391
  90.7 0.1 compare_convert_fusion
  90.8 0.0 collective-permute-done.5.refs_3_
  90.8 2.3 %cross_attention.1.refs_1_ = bf16[16,128,128]{2,1,0:T(8,128)(2,1)S(1)} custom-call(bf16[16,592,128]{2,1,0:T(8,128)(2,1)} %all-to-all-done.refs_1_.x_ref.refs_0_, bf16[16,592,128]{2,1,0:T(8,128)(2,1)} %all-to-all-done.refs_1_.x_ref.refs_0_, f32[416,256]{1,0:T(8,128)S(1)} %get-tuple-element.6.refs_2_.refs_1_, ...), custom_call_target="tpu_custom_call" | custom-call | flops 201326592 | bytes 1048576 | tf_op jit(solution)/shard_map/cross_attention/pallas_call | solution.py:268
  93.1 4.3 %self_attention.3 = bf16[16,64,128]{2,1,0:T(8,128)(2,1)S(1)} custom-call(bf16[16,384,128]{2,1,0:T(8,128)(2,1)} %all-to-all-done.1.refs_0_, bf16[16,128,128]{2,1,0:T(8,128)(2,1)S(1)} %cross_attention.1.refs_1_), custom_call_target="tpu_custom_call" | custom-call | flops 1073741824 | bytes 1572864 | tf_op jit(solution)/shard_map/self_attention/pallas_call | solution.py:151
  97.4 6.3 %collective-permute-done.6 = bf16[16,64,128]{2,1,0:T(8,128)(2,1)S(1)} collective-permute-done((bf16[16,64,128]{2,1,0:T(8,128)(2,1)S(1)}, bf16[16,64,128]{2,1,0:T(8,128)(2,1)S(1)}, u32[]{:S(2)}, u32[]{:S(2)}) %collective-permute-start.6) | collective-permute-done | bytes 262176 | tf_op jit(solution)/shard_map/ppermute | solution.py:391
  103.7 0.1 pad_maximum_fusion.1
  103.8 23.7 %all_to_all.15.x_ref = bf16[16,256,128]{2,1,0:T(8,128)(2,1)} all-to-all(bf16[16,256,128]{2,1,0:T(8,128)(2,1)S(1)} %pad_maximum_fusion.1), channel_id=1, replica_groups=mesh['y'=4,'zh'=2,'x'=4,'zl'=4,'c'=2] {'y','x'}, dimensions={0} | all-to-all | bytes 2097152 | tf_op jit(solution)/shard_map/all_to_all | solution.py:404
  127.5 2.0 %unpack.1 = (bf16[4,2,4,64,128]{4,3,2,1,0:T(8,128)(2,1)}, bf16[4,2,4,64,128]{4,3,2,1,0:T(8,128)(2,1)}) custom-call(s32[1]{0:T(128)} %bitcast.zh_ref, bf16[16,256,128]{2,1,0:T(8,128)(2,1)} %all_to_all.15.x_ref), custom_call_target="tpu_custom_call" | custom-call | tf_op jit(solution)/shard_map/unpack/pallas_call | solution.py:302
  (26 shorter events, 0.1 us)
Async XLA Ops:
  0.6 15.7 %copy-start = (bf16[128,2,32,128]{3,2,1,0:T(8,128)(2,1)S(1)}, bf16[128,2,32,128]{3,2,1,0:T(8,128)(2,1)}, u32[]{:S(2)}) copy-start(bf16[128,2,32,128]{3,2,1,0:T(8,128)(2,1)} %param.10) | copy-start | bytes 6291460
  0.6 7.6 %collective-permute-start.2 = (bf16[8,24,128]{2,1,0:T(8,128)(2,1)}, bf16[8,24,128]{2,1,0:T(8,128)(2,1)S(1)}, u32[]{:S(2)}, u32[]{:S(2)}) collective-permute-start(bf16[8,24,128]{2,1,0:T(8,128)(2,1)} %param.8), channel_id=1, source_target_pairs={{0,6},{2,0},{4,2},{6,4},{1,7},{3,1},{5,3},{7,5},{8,14},{10,8},{12,... | collective-permute-start | bytes 147464 | tf_op jit(solution)/shard_map/ppermute | solution.py:338
  5.9 4.9 %collective-permute-start = (bf16[8,24,128]{2,1,0:T(8,128)(2,1)}, bf16[8,24,128]{2,1,0:T(8,128)(2,1)S(1)}, u32[]{:S(2)}, u32[]{:S(2)}) collective-permute-start(bf16[8,24,128]{2,1,0:T(8,128)(2,1)} %param.8), channel_id=1, source_target_pairs={{0,2},{2,4},{4,6},{6,0},{1,3},{3,5},{5,7},{7,1},{8,10},{10,12},{12... | collective-permute-start | bytes 147464 | tf_op jit(solution)/shard_map/ppermute | solution.py:338
  5.9 5.0 %collective-permute-start.1 = (bf16[8,24,128]{2,1,0:T(8,128)(2,1)}, bf16[8,24,128]{2,1,0:T(8,128)(2,1)S(1)}, u32[]{:S(2)}, u32[]{:S(2)}) collective-permute-start(bf16[8,24,128]{2,1,0:T(8,128)(2,1)} %param.8), channel_id=1, source_target_pairs={{0,4},{2,6},{4,0},{6,2},{1,5},{3,7},{5,1},{7,3},{8,12},{10,14},{12... | collective-permute-start | bytes 147464 | tf_op jit(solution)/shard_map/ppermute | solution.py:338
  6.3 10.2 %copy-start.2 = (bf16[8,4,64,128]{3,2,1,0:T(8,128)(2,1)S(1)}, bf16[8,4,64,128]{3,2,1,0:T(8,128)(2,1)}, u32[]{:S(2)}) copy-start(bf16[8,4,64,128]{3,2,1,0:T(8,128)(2,1)} %param.7) | copy-start | bytes 1572868
  8.3 8.3 %copy-start.9 = (f32[128]{0:T(128)S(1)}, f32[128]{0:T(128)}, u32[]{:S(2)}) copy-start(f32[128]{0:T(128)} %param.9) | copy-start | bytes 1540
  8.3 8.3 %copy-start.6 = (bf16[8,24,128]{2,1,0:T(8,128)(2,1)S(1)}, bf16[8,24,128]{2,1,0:T(8,128)(2,1)}, u32[]{:S(2)}) copy-start(bf16[8,24,128]{2,1,0:T(8,128)(2,1)} %param.8) | copy-start | bytes 147460
  8.3 2.6 %copy-start.3 = (bf16[8,24,128]{2,1,0:T(8,128)(2,1)}, bf16[8,24,128]{2,1,0:T(8,128)(2,1)S(1)}, u32[]{:S(2)}) copy-start(bf16[8,24,128]{2,1,0:T(8,128)(2,1)S(1)} %collective-permute-done.2.refs_3_) | copy-start | bytes 147460
  10.8 0.6 copy-start.4
  11.5 0.6 copy-start.5
  12.1 38.8 %collective-permute-start.3 = (bf16[16,192,128]{2,1,0:T(8,128)(2,1)}, bf16[16,192,128]{2,1,0:T(8,128)(2,1)}, u32[]{:S(2)}, u32[]{:S(2)}) collective-permute-start(bf16[16,192,128]{2,1,0:T(8,128)(2,1)} %hold.2), channel_id=1, source_target_pairs={{0,32},{32,0},{1,33},{33,1},{2,34},{34,2},{3,35},{35,3},{4,36},{36... | collective-permute-start | bytes 2359304 | tf_op jit(solution)/shard_map/ppermute | solution.py:363
  19.4 36.4 %all-to-all-start = ((bf16[16,592,128]{2,1,0:T(8,128)(2,1)}), bf16[16,592,128]{2,1,0:T(8,128)(2,1)}, u32[]{:S(2)}, u32[]{:S(2)}) async-start(bf16[16,592,128]{2,1,0:T(8,128)(2,1)} %pad_maximum_fusion), calls=%async_computation | async-start | bytes 4849664 | tf_op jit(solution)/shard_map/all_to_all | solution.py:381
  55.9 29.1 %all-to-all-start.1 = ((bf16[16,384,128]{2,1,0:T(8,128)(2,1)}), bf16[16,384,128]{2,1,0:T(8,128)(2,1)}, u32[]{:S(2)}, u32[]{:S(2)}) async-start(bf16[16,384,128]{2,1,0:T(8,128)(2,1)} %hold.3.refs_0_), calls=%async_computation.1 | async-start | bytes 3145728 | tf_op jit(solution)/shard_map/all_to_all | solution.py:388
  64.2 4.4 %copy-start.10 = (s32[8]{0:T(128)S(1)}, s32[8]{0:T(128)}, u32[]{:S(2)}) copy-start(s32[8]{0:T(128)} %param.11) | copy-start | bytes 100
  66.3 4.0 %collective-permute-start.4 = (bf16[16,192,128]{2,1,0:T(8,128)(2,1)}, bf16[16,192,128]{2,1,0:T(8,128)(2,1)S(1)}, u32[]{:S(2)}, u32[]{:S(2)}) collective-permute-start(bf16[16,192,128]{2,1,0:T(8,128)(2,1)} %take.1.refs_1_), channel_id=1, source_target_pairs={{0,1},{1,0},{2,3},{3,2},{4,5},{5,4},{6,7},{7,6},{8,9},{9,8},{10,11... | collective-permute-start | bytes 2359304 | tf_op jit(solution)/shard_map/ppermute | solution.py:385
  70.3 1.1 copy-start.1
  74.1 16.6 %copy-start.7 = (s32[192]{0:T(256)S(1)}, s32[192]{0:T(256)}, u32[]{:S(2)}) copy-start(s32[192]{0:T(256)} %multiply_add_fusion) | copy-start | bytes 2308
  74.1 16.6 %copy-start.8 = (s32[2]{0:T(128)S(1)}, s32[2]{0:T(128)}, u32[]{:S(2)}) copy-start(s32[2]{0:T(128)} %dynamic_slice.7) | copy-start | bytes 28
  74.1 16.6 %collective-permute-start.5 = (bf16[480,256]{1,0:T(8,128)(2,1)S(1)}, bf16[480,256]{1,0:T(8,128)(2,1)S(1)}, u32[]{:S(2)}, u32[]{:S(2)}) collective-permute-start(bf16[480,256]{1,0:T(8,128)(2,1)S(1)} %get-tuple-element.7), channel_id=1, source_target_pairs={{0,32},{32,0},{1,33},{33,1},{2,34},{34,2},{3,35},{35,3},{4,36},{36... | collective-permute-start | bytes 737288 | tf_op jit(solution)/shard_map/ppermute | solution.py:387
  89.3 14.5 %collective-permute-start.6 = (bf16[16,64,128]{2,1,0:T(8,128)(2,1)S(1)}, bf16[16,64,128]{2,1,0:T(8,128)(2,1)S(1)}, u32[]{:S(2)}, u32[]{:S(2)}) collective-permute-start(bf16[16,64,128]{2,1,0:T(8,128)(2,1)S(1)} %self_attention.2), channel_id=1, source_target_pairs={{0,32},{32,0},{1,33},{33,1},{2,34},{34,2},{3,35},{35,3},{4,36},{36... | collective-permute-start | bytes 786440 | tf_op jit(solution)/shard_map/ppermute | solution.py:391

commit v5 on v4

--- a/solution.py
+++ b/solution.py
@@ -111,19 +111,16 @@
     )(buffer, *earlier)
 
 
-def self_kernel(from_far, x_ref, *refs):
+def self_kernel(*refs):
     o_ref = refs[-1]
     sources, local_len, head_size = o_ref.shape
     count = sources * local_len
     scale = head_size ** (-0.5) * log2e
 
-    def slot(k):
-        return x_ref[:, k * local_len : (k + 1) * local_len].reshape(count, head_size)
-
+    queries, *rest = (r[...].reshape(count, head_size) for r in refs[:5])
+    keys, given = rest[:2], rest[2:]
     ones = jnp.ones((count, head_size), jnp.bfloat16)
-    keys = [slot(1), slot(4)]
-    values = [jnp.concatenate([slot(k), ones], axis=1) for k in (2, 5)]
-    queries = slot(3 * from_far)
+    values = [jnp.concatenate([v, ones], axis=1) for v in given]
     block = 2
     for at in range(0, sources, block):
         some = queries[at * local_len : (at + block) * local_len]
@@ -144,7 +141,7 @@
     full_len = 2 * sources * local_len
 
     def kernel(*refs):
-        self_kernel(from_far, *refs)
+        self_kernel(*refs)
 
     room = local_len if into is None else into.shape[1]
     given = list(earlier) if into is None else [into] + list(earlier)
@@ -152,12 +149,15 @@
         kernel,
         out_shape=jax.ShapeDtypeStruct((sources, room, head_size), packed.dtype),
         grid=(1,),
-        in_specs=[whole(packed)]
+        in_specs=[
+            pl.BlockSpec((sources, local_len, head_size), lambda i, k=k: (0, k, 0))
+            for k in (3 * from_far, 1, 4, 2, 5)
+        ]
         + [pl.BlockSpec(memory_space=pl.ANY)] * len(given),
         out_specs=pl.BlockSpec(
             (sources, local_len, head_size), lambda i: (0, room // local_len - 1, 0)
         ),
-        input_output_aliases={} if into is None else {1: 0},
+        input_output_aliases={} if into is None else {5: 0},
         compiler_params=params(),
         cost_estimate=pl.CostEstimate(
             flops=2 * full_len * full_len * head_size,
@@ -165,7 +165,7 @@
             transcendentals=full_len * full_len // 2,
         ),
         name="self_attention",
-    )(packed, *given)
+    )(*[packed] * 5, *given)
 
 
 def project_kernel(w_first, got_ref, mine_ref, other_ref, part_ref, sent_ref):

time: 130 us -> 130 us (level)
  no operation moved by 1% of the time
where the time goes in v5:
time: 130 us; the launch traced here: 129 us
  waiting for transfers between devices  46.4 us (36%)
  starting transfers between devices  29.5 us (23%)
  blocking collectives  23.7 us (18%)
  Pallas kernels  21.9 us (17%)
  local copies, waits for them, and re-layouts  3.96 us (3%)
  other arithmetic  3.19 us (2%)
    ppermute x1, waiting for transfers between devices, body(): far = lax.ppermute(hold(far, rows[1:]), 'zh', SWAP)  24.6 us
    all_to_all x1, blocking collectives, body(): outs = lax.all_to_all(outs, XY, split_axis=0, concat_axis=0, tiled=True)  23.7 us
    all_to_all x1, waiting for transfers between devices, body(): packed = lax.all_to_all(packed, XY, split_axis=0, concat_axis=0, tiled=True)  9.6 us
    pallas_call x2, Pallas kernels, self_attention(): pl.pallas_call(kernel, out_shape=jax.ShapeDtypeStruct((sources, room, hea...  8.38 us
    all_to_all x1, starting transfers between devices, body(): packed = lax.all_to_all(packed, XY, split_axis=0, concat_axis=0, tiled=True)  8.3 us
    all_to_all x1, starting transfers between devices, body(): got = lax.all_to_all(sent, XY, split_axis=0, concat_axis=0, tiled=True)  6.8 us
    ppermute x1, waiting for transfers between devices, body(): far_out = lax.ppermute(far_out, 'zh', SWAP)  6.46 us
    ppermute x3, starting transfers between devices, ahead(): return lax.ppermute(value, axis, [(i, (i + step) % 4) for i in range(4)])  5.63 us
  transfers between devices with their start and end apart: 9, of which 6 were waited for; matrix products, arithmetic and copies ran while one was open for 4% of the time, Pallas kernels for 15%

profile of v5, /device:TPU:1, one launch (start us, length us, event | category | flops | bytes accessed | tf_op | source)
XLA Modules:
  0.0 129.4 jit_solution(4971729694928849788)
XLA Ops:
  0.6 0.0 copy-start
  0.6 5.3 %collective-permute-start.2 = (bf16[8,24,128]{2,1,0:T(8,128)(2,1)}, bf16[8,24,128]{2,1,0:T(8,128)(2,1)S(1)}, u32[]{:S(2)}, u32[]{:S(2)}) collective-permute-start(bf16[8,24,128]{2,1,0:T(8,128)(2,1)} %param.8), channel_id=1, source_target_pairs={{0,6},{2,0},{4,2},{6,4},{1,7},{3,1},{5,3},{7,5},{8,14},{10,8},{12,... | collective-permute-start | bytes 147464 | tf_op jit(solution)/shard_map/ppermute | solution.py:338
  5.9 0.0 collective-permute-start
  5.9 0.4 collective-permute-start.1
  6.3 2.0 %pick.1.refs_0_ = bf16[16,192,128]{2,1,0:T(8,128)(2,1)} custom-call(s32[1]{0:T(128)S(6)} %sub.21.zh_ref, bf16[4,2,4,192,128]{4,3,2,1,0:T(8,128)(2,1)} %bitcast.37), custom_call_target="tpu_custom_call" | custom-call | tf_op jit(solution)/shard_map/pick/pallas_call | solution.py:49
  8.3 0.0 collective-permute-done.2.refs_3_
  8.3 0.0 copy-start.3
  8.3 2.6 %collective-permute-done.refs_1_ = bf16[8,24,128]{2,1,0:T(8,128)(2,1)S(1)} collective-permute-done((bf16[8,24,128]{2,1,0:T(8,128)(2,1)}, bf16[8,24,128]{2,1,0:T(8,128)(2,1)S(1)}, u32[]{:S(2)}, u32[]{:S(2)}) %collective-permute-start) | collective-permute-done | bytes 49184 | tf_op jit(solution)/shard_map/ppermute | solution.py:338
  10.8 0.0 collective-permute-done.1.refs_2_
  10.9 0.0 copy-done.3
  10.9 0.6 copy-done.4
  11.5 0.6 copy-done.5
  12.1 4.2 %collective-permute-start.3 = (bf16[16,192,128]{2,1,0:T(8,128)(2,1)}, bf16[16,192,128]{2,1,0:T(8,128)(2,1)}, u32[]{:S(2)}, u32[]{:S(2)}) collective-permute-start(bf16[16,192,128]{2,1,0:T(8,128)(2,1)} %hold.2), channel_id=1, source_target_pairs={{0,32},{32,0},{1,33},{33,1},{2,34},{34,2},{3,35},{35,3},{4,36},{36... | collective-permute-start | bytes 2359304 | tf_op jit(solution)/shard_map/ppermute | solution.py:363
  16.3 0.1 constant_dynamic-slice_fusion
  16.6 0.9 pad_maximum_fusion.2
  17.5 0.2 broadcast_in_dim.48
  17.7 0.1 broadcast_in_dim.46
  17.9 1.6 %pad_maximum_fusion = bf16[16,592,128]{2,1,0:T(8,128)(2,1)} fusion(bf16[16,16,128]{2,1,0:T(8,128)(2,1)S(1)} %broadcast_in_dim.49, bf16[16,256,128]{2,1,0:T(8,128)(2,1)S(1)} %bitcast.34, bf16[16,192,128]{2,1,0:T(8,128)(2,1)S(1)} %bitcast.35, bf16[16,128,128]{2,1,0:T(8,128)(2,1)S(1)} %bitcast.36), kind=kLoop, calls=%fused_computation | loop fusion | flops 9699328 | bytes 4849664 | tf_op jit(solution)/shard_map/concatenate | solution.py:372
  19.4 6.8 %all-to-all-start = ((bf16[16,592,128]{2,1,0:T(8,128)(2,1)}), bf16[16,592,128]{2,1,0:T(8,128)(2,1)}, u32[]{:S(2)}, u32[]{:S(2)}) async-start(bf16[16,592,128]{2,1,0:T(8,128)(2,1)} %pad_maximum_fusion), calls=%async_computation | async-start | bytes 4849664 | tf_op jit(solution)/shard_map/all_to_all | solution.py:381
  26.2 24.6 %collective-permute-done.3.far_ref = bf16[16,192,128]{2,1,0:T(8,128)(2,1)} collective-permute-done((bf16[16,192,128]{2,1,0:T(8,128)(2,1)}, bf16[16,192,128]{2,1,0:T(8,128)(2,1)}, u32[]{:S(2)}, u32[]{:S(2)}) %collective-permute-start.3) | collective-permute-done | bytes 786464 | tf_op jit(solution)/shard_map/ppermute | solution.py:363
  50.9 2.4 %build.1.refs_0_ = bf16[16,384,128]{2,1,0:T(8,128)(2,1)} custom-call(s32[1]{0:T(128)} %bitcast.zh_ref, bf16[4,2,4,192,128]{4,3,2,1,0:T(8,128)(2,1)} %bitcast.38, bf16[16,192,128]{2,1,0:T(8,128)(2,1)} %collective-permute-done.3.far_ref), custom_call_target="tpu_custom_call" | custom-call | flops 99999997952 | bytes 3145728 | tf_op jit(solution)/shard_map/build/pallas_call | solution.py:75
  53.2 2.6 %all-to-all-done.refs_1_.x_ref.refs_0_ = bf16[16,592,128]{2,1,0:T(8,128)(2,1)} async-done(((bf16[16,592,128]{2,1,0:T(8,128)(2,1)}), bf16[16,592,128]{2,1,0:T(8,128)(2,1)}, u32[]{:S(2)}, u32[]{:S(2)}) %all-to-all-start) | async-done | bytes 2424864 | tf_op jit(solution)/shard_map/all_to_all | solution.py:381
  55.9 8.3 %all-to-all-start.1 = ((bf16[16,384,128]{2,1,0:T(8,128)(2,1)}), bf16[16,384,128]{2,1,0:T(8,128)(2,1)}, u32[]{:S(2)}, u32[]{:S(2)}) async-start(bf16[16,384,128]{2,1,0:T(8,128)(2,1)} %hold.3.refs_0_), calls=%async_computation.1 | async-start | bytes 3145728 | tf_op jit(solution)/shard_map/all_to_all | solution.py:388
  64.2 0.0 copy-start.10
  64.2 2.1 %take.1.refs_1_ = bf16[16,192,128]{2,1,0:T(8,128)(2,1)} custom-call(bf16[16,592,128]{2,1,0:T(8,128)(2,1)} %all-to-all-done.refs_1_.x_ref.refs_0_, bf16[16,384,128]{2,1,0:T(8,128)(2,1)} %hold.3.refs_0_), custom_call_target="tpu_custom_call" | custom-call | tf_op jit(solution)/shard_map/take/pallas_call | solution.py:103
  66.3 1.9 %collective-permute-start.4 = (bf16[16,192,128]{2,1,0:T(8,128)(2,1)}, bf16[16,192,128]{2,1,0:T(8,128)(2,1)S(1)}, u32[]{:S(2)}, u32[]{:S(2)}) collective-permute-start(bf16[16,192,128]{2,1,0:T(8,128)(2,1)} %take.1.refs_1_), channel_id=1, source_target_pairs={{0,1},{1,0},{2,3},{3,2},{4,5},{5,4},{6,7},{7,6},{8,9},{9,8},{10,11... | collective-permute-start | bytes 2359304 | tf_op jit(solution)/shard_map/ppermute | solution.py:385
  68.2 0.1 broadcast_in_dim.54
  68.3 0.1 select_n.32
  68.4 0.1 broadcast_in_dim.50
  68.4 0.1 broadcast_in_dim.51
  68.5 0.1 broadcast_in_dim.56
  68.6 0.6 dynamic_slice.7
  69.2 0.6 multiply_add_fusion
  69.8 0.5 collective-permute-done.4.refs_2_
  70.3 1.1 copy-done.1
  71.5 2.7 %project.1 = (f32[416,256]{1,0:T(8,128)S(1)}, bf16[480,256]{1,0:T(8,128)(2,1)S(1)}) custom-call(bf16[16,592,128]{2,1,0:T(8,128)(2,1)} %all-to-all-done.refs_1_.x_ref.refs_0_, bf16[16,192,128]{2,1,0:T(8,128)(2,1)S(1)} %copy-done.1, bf16[16,192,128]{2,1,0:T(8,128)(2,1)S(1)} %collective-permute-done.4.refs_2_), custom_call_target="tpu_custom_call" | custom-call | flops 402653184 | bytes 4849664 | tf_op jit(solution)/shard_map/project/pallas_call | solution.py:209
  74.1 1.2 collective-permute-start.5
  75.4 9.6 %all-to-all-done.1.refs_0_.refs_1_.refs_2_.refs_3_.refs_4_ = bf16[16,384,128]{2,1,0:T(8,128)(2,1)} async-done(((bf16[16,384,128]{2,1,0:T(8,128)(2,1)}), bf16[16,384,128]{2,1,0:T(8,128)(2,1)}, u32[]{:S(2)}, u32[]{:S(2)}) %all-to-all-start.1) | async-done | bytes 1572896 | tf_op jit(solution)/shard_map/all_to_all | solution.py:388
  85.0 4.2 %self_attention.2 = bf16[16,64,128]{2,1,0:T(8,128)(2,1)S(1)} custom-call(bf16[16,384,128]{2,1,0:T(8,128)(2,1)} %all-to-all-done.1.refs_0_.refs_1_.refs_2_.refs_3_.refs_4_, bf16[16,384,128]{2,1,0:T(8,128)(2,1)} %all-to-all-done.1.refs_0_.refs_1_.refs_2_.refs_3_.refs_4_, bf16[16,384,128]{2,1,0:T(8,128)(2,1)} %all-to-all-done.1.refs_0_.refs_1_.refs_2_.refs_3_.refs_4_, ...), custom_call_target="tpu_custom_call" | custom-call | flops 1073741824 | bytes 1572864 | tf_op jit(solution)/shard_map/self_attention/pallas_call | solution.py:148
  89.2 1.4 %collective-permute-start.6 = (bf16[16,64,128]{2,1,0:T(8,128)(2,1)S(1)}, bf16[16,64,128]{2,1,0:T(8,128)(2,1)S(1)}, u32[]{:S(2)}, u32[]{:S(2)}) collective-permute-start(bf16[16,64,128]{2,1,0:T(8,128)(2,1)S(1)} %self_attention.2), channel_id=1, source_target_pairs={{0,32},{32,0},{1,33},{33,1},{2,34},{34,2},{3,35},{35,3},{4,36},{36... | collective-permute-start | bytes 786440 | tf_op jit(solution)/shard_map/ppermute | solution.py:391
  90.6 0.1 compare_convert_fusion
  90.7 0.0 collective-permute-done.5.refs_3_
  90.7 2.3 %cross_attention.1.refs_5_ = bf16[16,128,128]{2,1,0:T(8,128)(2,1)S(1)} custom-call(bf16[16,592,128]{2,1,0:T(8,128)(2,1)} %all-to-all-done.refs_1_.x_ref.refs_0_, bf16[16,592,128]{2,1,0:T(8,128)(2,1)} %all-to-all-done.refs_1_.x_ref.refs_0_, f32[416,256]{1,0:T(8,128)S(1)} %get-tuple-element.6.refs_2_.refs_5_, ...), custom_call_target="tpu_custom_call" | custom-call | flops 201326592 | bytes 1048576 | tf_op jit(solution)/shard_map/cross_attention/pallas_call | solution.py:268
  93.0 4.2 %self_attention.3 = bf16[16,64,128]{2,1,0:T(8,128)(2,1)S(1)} custom-call(bf16[16,384,128]{2,1,0:T(8,128)(2,1)} %all-to-all-done.1.refs_0_.refs_1_.refs_2_.refs_3_.refs_4_, bf16[16,384,128]{2,1,0:T(8,128)(2,1)} %all-to-all-done.1.refs_0_.refs_1_.refs_2_.refs_3_.refs_4_, bf16[16,384,128]{2,1,0:T(8,128)(2,1)} %all-to-all-done.1.refs_0_.refs_1_.refs_2_.refs_3_.refs_4_, ...), custom_call_target="tpu_custom_call" | custom-call | flops 1073741824 | bytes 1572864 | tf_op jit(solution)/shard_map/self_attention/pallas_call | solution.py:148
  97.2 6.5 %collective-permute-done.6 = bf16[16,64,128]{2,1,0:T(8,128)(2,1)S(1)} collective-permute-done((bf16[16,64,128]{2,1,0:T(8,128)(2,1)S(1)}, bf16[16,64,128]{2,1,0:T(8,128)(2,1)S(1)}, u32[]{:S(2)}, u32[]{:S(2)}) %collective-permute-start.6) | collective-permute-done | bytes 262176 | tf_op jit(solution)/shard_map/ppermute | solution.py:391
  103.6 0.1 pad_maximum_fusion.1
  103.7 23.7 %all_to_all.15.x_ref = bf16[16,256,128]{2,1,0:T(8,128)(2,1)} all-to-all(bf16[16,256,128]{2,1,0:T(8,128)(2,1)S(1)} %pad_maximum_fusion.1), channel_id=1, replica_groups=mesh['y'=4,'zh'=2,'x'=4,'zl'=4,'c'=2] {'y','x'}, dimensions={0} | all-to-all | bytes 2097152 | tf_op jit(solution)/shard_map/all_to_all | solution.py:404
  127.4 2.0 %unpack.1 = (bf16[4,2,4,64,128]{4,3,2,1,0:T(8,128)(2,1)}, bf16[4,2,4,64,128]{4,3,2,1,0:T(8,128)(2,1)}) custom-call(s32[1]{0:T(128)} %bitcast.zh_ref, bf16[16,256,128]{2,1,0:T(8,128)(2,1)} %all_to_all.15.x_ref), custom_call_target="tpu_custom_call" | custom-call | tf_op jit(solution)/shard_map/unpack/pallas_call | solution.py:302
  (26 shorter events, 0.1 us)
Async XLA Ops:
  0.6 15.7 %copy-start = (bf16[128,2,32,128]{3,2,1,0:T(8,128)(2,1)S(1)}, bf16[128,2,32,128]{3,2,1,0:T(8,128)(2,1)}, u32[]{:S(2)}) copy-start(bf16[128,2,32,128]{3,2,1,0:T(8,128)(2,1)} %param.10) | copy-start | bytes 6291460
  0.6 7.6 %collective-permute-start.2 = (bf16[8,24,128]{2,1,0:T(8,128)(2,1)}, bf16[8,24,128]{2,1,0:T(8,128)(2,1)S(1)}, u32[]{:S(2)}, u32[]{:S(2)}) collective-permute-start(bf16[8,24,128]{2,1,0:T(8,128)(2,1)} %param.8), channel_id=1, source_target_pairs={{0,6},{2,0},{4,2},{6,4},{1,7},{3,1},{5,3},{7,5},{8,14},{10,8},{12,... | collective-permute-start | bytes 147464 | tf_op jit(solution)/shard_map/ppermute | solution.py:338
  5.9 4.9 %collective-permute-start = (bf16[8,24,128]{2,1,0:T(8,128)(2,1)}, bf16[8,24,128]{2,1,0:T(8,128)(2,1)S(1)}, u32[]{:S(2)}, u32[]{:S(2)}) collective-permute-start(bf16[8,24,128]{2,1,0:T(8,128)(2,1)} %param.8), channel_id=1, source_target_pairs={{0,2},{2,4},{4,6},{6,0},{1,3},{3,5},{5,7},{7,1},{8,10},{10,12},{12... | collective-permute-start | bytes 147464 | tf_op jit(solution)/shard_map/ppermute | solution.py:338
  5.9 5.0 %collective-permute-start.1 = (bf16[8,24,128]{2,1,0:T(8,128)(2,1)}, bf16[8,24,128]{2,1,0:T(8,128)(2,1)S(1)}, u32[]{:S(2)}, u32[]{:S(2)}) collective-permute-start(bf16[8,24,128]{2,1,0:T(8,128)(2,1)} %param.8), channel_id=1, source_target_pairs={{0,4},{2,6},{4,0},{6,2},{1,5},{3,7},{5,1},{7,3},{8,12},{10,14},{12... | collective-permute-start | bytes 147464 | tf_op jit(solution)/shard_map/ppermute | solution.py:338
  6.3 10.2 %copy-start.2 = (bf16[8,4,64,128]{3,2,1,0:T(8,128)(2,1)S(1)}, bf16[8,4,64,128]{3,2,1,0:T(8,128)(2,1)}, u32[]{:S(2)}) copy-start(bf16[8,4,64,128]{3,2,1,0:T(8,128)(2,1)} %param.7) | copy-start | bytes 1572868
  8.3 8.3 %copy-start.9 = (f32[128]{0:T(128)S(1)}, f32[128]{0:T(128)}, u32[]{:S(2)}) copy-start(f32[128]{0:T(128)} %param.9) | copy-start | bytes 1540
  8.3 8.3 %copy-start.6 = (bf16[8,24,128]{2,1,0:T(8,128)(2,1)S(1)}, bf16[8,24,128]{2,1,0:T(8,128)(2,1)}, u32[]{:S(2)}) copy-start(bf16[8,24,128]{2,1,0:T(8,128)(2,1)} %param.8) | copy-start | bytes 147460
  8.3 2.6 %copy-start.3 = (bf16[8,24,128]{2,1,0:T(8,128)(2,1)}, bf16[8,24,128]{2,1,0:T(8,128)(2,1)S(1)}, u32[]{:S(2)}) copy-start(bf16[8,24,128]{2,1,0:T(8,128)(2,1)S(1)} %collective-permute-done.2.refs_3_) | copy-start | bytes 147460
  10.8 0.6 copy-start.4
  11.5 0.6 copy-start.5
  12.1 38.8 %collective-permute-start.3 = (bf16[16,192,128]{2,1,0:T(8,128)(2,1)}, bf16[16,192,128]{2,1,0:T(8,128)(2,1)}, u32[]{:S(2)}, u32[]{:S(2)}) collective-permute-start(bf16[16,192,128]{2,1,0:T(8,128)(2,1)} %hold.2), channel_id=1, source_target_pairs={{0,32},{32,0},{1,33},{33,1},{2,34},{34,2},{3,35},{35,3},{4,36},{36... | collective-permute-start | bytes 2359304 | tf_op jit(solution)/shard_map/ppermute | solution.py:363
  19.4 36.4 %all-to-all-start = ((bf16[16,592,128]{2,1,0:T(8,128)(2,1)}), bf16[16,592,128]{2,1,0:T(8,128)(2,1)}, u32[]{:S(2)}, u32[]{:S(2)}) async-start(bf16[16,592,128]{2,1,0:T(8,128)(2,1)} %pad_maximum_fusion), calls=%async_computation | async-start | bytes 4849664 | tf_op jit(solution)/shard_map/all_to_all | solution.py:381
  55.9 29.1 %all-to-all-start.1 = ((bf16[16,384,128]{2,1,0:T(8,128)(2,1)}), bf16[16,384,128]{2,1,0:T(8,128)(2,1)}, u32[]{:S(2)}, u32[]{:S(2)}) async-start(bf16[16,384,128]{2,1,0:T(8,128)(2,1)} %hold.3.refs_0_), calls=%async_computation.1 | async-start | bytes 3145728 | tf_op jit(solution)/shard_map/all_to_all | solution.py:388
  64.2 4.4 %copy-start.10 = (s32[8]{0:T(128)S(1)}, s32[8]{0:T(128)}, u32[]{:S(2)}) copy-start(s32[8]{0:T(128)} %param.11) | copy-start | bytes 100
  66.3 4.0 %collective-permute-start.4 = (bf16[16,192,128]{2,1,0:T(8,128)(2,1)}, bf16[16,192,128]{2,1,0:T(8,128)(2,1)S(1)}, u32[]{:S(2)}, u32[]{:S(2)}) collective-permute-start(bf16[16,192,128]{2,1,0:T(8,128)(2,1)} %take.1.refs_1_), channel_id=1, source_target_pairs={{0,1},{1,0},{2,3},{3,2},{4,5},{5,4},{6,7},{7,6},{8,9},{9,8},{10,11... | collective-permute-start | bytes 2359304 | tf_op jit(solution)/shard_map/ppermute | solution.py:385
  70.3 1.1 copy-start.1
  74.1 16.6 %collective-permute-start.5 = (bf16[480,256]{1,0:T(8,128)(2,1)S(1)}, bf16[480,256]{1,0:T(8,128)(2,1)S(1)}, u32[]{:S(2)}, u32[]{:S(2)}) collective-permute-start(bf16[480,256]{1,0:T(8,128)(2,1)S(1)} %get-tuple-element.7), channel_id=1, source_target_pairs={{0,32},{32,0},{1,33},{33,1},{2,34},{34,2},{3,35},{35,3},{4,36},{36... | collective-permute-start | bytes 737288 | tf_op jit(solution)/shard_map/ppermute | solution.py:387
  85.0 5.6 %copy-start.7 = (s32[192]{0:T(256)S(1)}, s32[192]{0:T(256)}, u32[]{:S(2)}) copy-start(s32[192]{0:T(256)} %multiply_add_fusion) | copy-start | bytes 2308
  85.0 5.6 %copy-start.8 = (s32[2]{0:T(128)S(1)}, s32[2]{0:T(128)}, u32[]{:S(2)}) copy-start(s32[2]{0:T(128)} %dynamic_slice.7) | copy-start | bytes 28
  89.2 14.5 %collective-permute-start.6 = (bf16[16,64,128]{2,1,0:T(8,128)(2,1)S(1)}, bf16[16,64,128]{2,1,0:T(8,128)(2,1)S(1)}, u32[]{:S(2)}, u32[]{:S(2)}) collective-permute-start(bf16[16,64,128]{2,1,0:T(8,128)(2,1)S(1)} %self_attention.2), channel_id=1, source_target_pairs={{0,32},{32,0},{1,33},{33,1},{2,34},{34,2},{3,35},{35,3},{4,36},{36... | collective-permute-start | bytes 786440 | tf_op jit(solution)/shard_map/ppermute | solution.py:391
